TPU v7x, 32 devices: a whole 2x2x4 slice. The times are simulated.
32 devices in a mesh: dp: 4 (over z), fsdp: 8 (over y, x, core).
Axes of the slice: x: 2, y: 2, z: 4, core: 2. Of those that a mesh axis runs over, the one named last changes fastest.
Arguments:
- out_grad: bfloat16 [256, 4096], P(('dp', 'fsdp')), may hold values from -6 to 6
- gate_pre: bfloat16 [256, 14848], P('dp', 'fsdp'), may hold values from -6 to 6
- up_pre: bfloat16 [256, 14848], P('dp', 'fsdp'), may hold values from -6 to 6
- down_weight: bfloat16 [14848, 4096], P('fsdp', 'dp'), may hold values from -0.09375 to 0.09375
- momentum: float32 [4, 14848, 256], P('dp', 'fsdp'), may hold values from -6 to 6
- band_index: int32 [4, 14848, 32], P('dp', 'fsdp'), may hold values from 0 to 255, as said below
- band_count: int32 [4, 14848], P('dp', 'fsdp'), may hold values from 1 to 32, as said below
Outputs:
- gate_grad: bfloat16 [256, 14848], P('dp', 'fsdp')
- up_grad: bfloat16 [256, 14848], P('dp', 'fsdp')
- new_momentum: float32 [4, 14848, 256], P('dp', 'fsdp')
- update: float32 [14848, 256], P('fsdp')
Inputs may be any that keep to these rules, and one draw needn't show every extreme that they name: `band_index`: for each worker and block the 32 entries of the list are different frequencies. `band_count`: on every worker some block uses all 32 entries and some block uses one.
All inputs are finite; a program needn't handle non-finite values.
Results may differ from a plain program's by a relative error of at most 0.0019.
Values may be sent and summed in bfloat16 or wider, within the bound.
A program may use at most 64 MiB of HBM per device.

v0:
```python
import math

import jax
import jax.numpy as jnp
from jax import lax
from jax.sharding import PartitionSpec as P

momentum_decay = 0.9


def cosine_matrix(length):
    frequency = jnp.arange(length, dtype=jnp.int32).astype(jnp.float32)[:, None]
    position = jnp.arange(length, dtype=jnp.int32).astype(jnp.float32)[None, :]
    angles = math.pi * (position + 0.5) * frequency / length
    row_weight = jnp.where(frequency == 0.0, math.sqrt(1.0 / length), math.sqrt(2.0 / length))
    return jnp.cos(angles) * row_weight


def per_device(out_grad, gate_pre, up_pre, down_weight, momentum, band_index, band_count):
    worker_rows = gate_pre.shape[0]
    own_rows = gate_pre.shape[1]
    window = momentum.shape[2]
    workers = lax.axis_size("dp")
    gate_float = gate_pre.astype(jnp.float32)
    up_float = up_pre.astype(jnp.float32)
    sigmoid_gate = jax.nn.sigmoid(gate_float)
    activation = gate_float * sigmoid_gate
    hidden = (activation * up_float).astype(jnp.bfloat16)
    contract_last = (((1,), (1,)), ((), ()))
    all_grad = lax.all_gather(out_grad, "fsdp", axis=0, tiled=True)
    hidden_grad = lax.dot_general(
        all_grad,
        lax.all_gather(down_weight, "dp", axis=1, tiled=True),
        contract_last,
        preferred_element_type=jnp.float32,
    )
    window_grad = all_grad[:, :window]
    up_grad = (hidden_grad * activation).astype(jnp.bfloat16)
    gate_grad = (
        hidden_grad * up_float * sigmoid_gate * (1.0 + gate_float * (1.0 - sigmoid_gate))
    ).astype(jnp.bfloat16)
    grad_scale = 1.0 / math.sqrt(worker_rows)
    worker_grad = (
        lax.dot_general(
            hidden, window_grad, (((0,), (0,)), ((), ())), preferred_element_type=jnp.float32
        )
        * grad_scale
    )
    block_count = band_index.shape[1]
    slot_count = band_index.shape[2]
    length = own_rows * window // block_count
    cosine_table = cosine_matrix(length)
    momentum_mixed = momentum_decay * momentum[0] + worker_grad
    spectrum = jnp.dot(momentum_mixed, cosine_table.T, precision=lax.Precision.HIGHEST)
    slot_list = band_index[0]
    slot_ids = jnp.arange(slot_count, dtype=jnp.int32)
    picked = jnp.take_along_axis(spectrum, slot_list, axis=1)
    band_values = jnp.where(slot_ids[None, :] < band_count[0][:, None], picked, 0.0)
    frequency = jnp.arange(length, dtype=jnp.int32)
    own_spectrum = jnp.sum(
        jnp.where(slot_list[:, :, None] == frequency[None, None, :], band_values[:, :, None], 0.0),
        axis=1,
    )
    momentum_kept = momentum_mixed - jnp.dot(
        own_spectrum, cosine_table, precision=lax.Precision.HIGHEST
    )
    frequency_float = frequency.astype(jnp.float32)
    running = jnp.zeros((block_count, length), jnp.float32)

    def one_worker(partial_sum, member_pair):
        worker_values, worker_places = member_pair
        matches = worker_places[:, :, None] == frequency_float[None, None, :]
        return (
            partial_sum + jnp.sum(jnp.where(matches, worker_values[:, :, None], 0.0), axis=1),
            None,
        )

    running, _ = lax.scan(
        one_worker,
        running,
        (
            lax.all_gather(band_values[None], "dp", axis=0, tiled=True),
            lax.all_gather(slot_list.astype(jnp.float32)[None], "dp", axis=0, tiled=True),
        ),
    )
    update = jnp.dot(running / workers, cosine_table, precision=lax.Precision.HIGHEST)
    new_momentum = momentum_kept[None]
    return (gate_grad, up_grad, new_momentum, update)


def solution(mesh):
    placed = (
        P(("dp", "fsdp"), None),
        P("dp", "fsdp"),
        P("dp", "fsdp"),
        P("fsdp", "dp"),
        P("dp", "fsdp", None),
        P("dp", "fsdp", None),
        P("dp", "fsdp"),
    )
    return jax.shard_map(
        per_device,
        mesh=mesh,
        in_specs=placed,
        out_specs=(P("dp", "fsdp"), P("dp", "fsdp"), P("dp", "fsdp", None), P("fsdp", None)),
        check_vma=False,
    )
```

profile of v0, /device:TPU:0, one launch (start us, length us, event | category | flops | bytes accessed | tf_op | source)
XLA Modules:
  0.0 715.8 jit_solution(17781731912226712384)
XLA Ops:
  10.8 11.3 %all_gather.12 = bf16[64,4096]{1,0:T(8,128)(2,1)S(1)} all-gather(bf16[8,4096]{1,0:T(8,128)(2,1)S(1)} %copy-done.10), channel_id=1, replica_groups=mesh['dp'=4,'fsdp'=8] {'fsdp'}, dimensions={0}, use_global_device_ids=true | all-gather | bytes 589824 | tf_op jit(solution)/shard_map/all_gather | solution.py:30
  22.1 1.9 fusion.2
  25.3 2.7 fusion.15
  27.9 468.0 %gather_fusion = f32[59392]{0:T(1024)S(1)} fusion(f32[1856,256]{1,0:T(8,128)S(1)} %fusion.15, s32[59392]{0:T(1024)S(1)} %reshape.143), kind=kCustom, calls=%fused_computation | custom fusion | bytes 950272 | tf_op jit(solution)/shard_map/jit(take_along_axis)/gather | solution.py:57
  498.4 1.5 copy.36
  500.2 20.6 %select_reduce_fusion.1 = f32[1856,256]{1,0:T(8,128)S(1)} fusion(f32[1856,32]{1,0:T(8,128)S(1)} %select_select_fusion.1, s32[1856,32]{1,0:T(8,128)S(1)} %bitcast.22), kind=kLoop, calls=%fused_computation.7 | loop fusion | flops 45137920 | bytes 2375680 | tf_op jit(solution)/shard_map/reduce_sum | solution.py:60
  520.8 3.9 fusion.3
  524.7 22.4 %all_gather.14 = f32[4,1856,32]{1,2,0:T(8,128)} all-gather(f32[1,1856,32]{1,2,0:T(8,128)S(1)} %copy-done.7), channel_id=1, replica_groups=mesh['dp'=4,'fsdp'=8] {'dp'}, dimensions={0}, use_global_device_ids=true | all-gather | bytes 1187840 | tf_op jit(solution)/shard_map/all_gather | solution.py:83
  547.1 21.5 %all_gather.15 = f32[4,1856,32]{1,2,0:T(8,128)} all-gather(f32[1,1856,32]{1,2,0:T(8,128)S(1)} %copy.36), channel_id=1, replica_groups=mesh['dp'=4,'fsdp'=8] {'dp'}, dimensions={0}, use_global_device_ids=true | all-gather | bytes 1187840 | tf_op jit(solution)/shard_map/all_gather | solution.py:82
  568.6 124.0 %while.11 = (s32[]{:T(128)}, f32[1856,256]{1,0:T(8,128)}, f32[4,1856,32]{1,2,0:T(8,128)}, f32[4,1856,32]{1,2,0:T(8,128)}, s32[]{:T(128)}, /*index=5*/s32[]{:T(128)}) while((s32[]{:T(128)}, f32[1856,256]{1,0:T(8,128)}, f32[4,1856,32]{1,2,0:T(8,128)}, f32[4,1856,32]{1,2,0:T(8,128)}, s32[]{:T(128)}, /*index=5*/s32[]{:T(128)}) %tuple.33), condition=%wide.region_3.4_spmd.clone, body=%wide.region_1.3_spmd.clone.sunk | while | flops 46088448 | bytes 9979995 | solution.py:78
  570.1 1.3 copy.44
  571.3 25.7 %select_reduce_fusion.3 = f32[1856,256]{1,0:T(8,128)S(1)} fusion(f32[1856,32]{1,0:T(8,128)S(1)} %bitcast.20, f32[256]{0:T(256)S(1)} %iota_convert_fusion.3, f32[1856,32]{1,0:T(8,128)} %bitcast.21), kind=kLoop, calls=%fused_computation.2.clone.1 | loop fusion | flops 45137920 | bytes 2376704 | tf_op jit(solution)/shard_map/while/body/eval_jaxpr/reduce_sum | solution.py:74
  597.0 1.5 select_add_fusion.2
  599.9 1.3 copy.44
  601.2 25.7 %select_reduce_fusion.3 = f32[1856,256]{1,0:T(8,128)S(1)} fusion(f32[1856,32]{1,0:T(8,128)S(1)} %bitcast.20, f32[256]{0:T(256)S(1)} %iota_convert_fusion.3, f32[1856,32]{1,0:T(8,128)} %bitcast.21), kind=kLoop, calls=%fused_computation.2.clone.1 | loop fusion | flops 45137920 | bytes 2376704 | tf_op jit(solution)/shard_map/while/body/eval_jaxpr/reduce_sum | solution.py:74
  626.9 3.0 select_add_fusion.2
  631.3 1.3 copy.44
  632.6 25.7 %select_reduce_fusion.3 = f32[1856,256]{1,0:T(8,128)S(1)} fusion(f32[1856,32]{1,0:T(8,128)S(1)} %bitcast.20, f32[256]{0:T(256)S(1)} %iota_convert_fusion.3, f32[1856,32]{1,0:T(8,128)} %bitcast.21), kind=kLoop, calls=%fused_computation.2.clone.1 | loop fusion | flops 45137920 | bytes 2376704 | tf_op jit(solution)/shard_map/while/body/eval_jaxpr/reduce_sum | solution.py:74
  658.2 3.0 select_add_fusion.2
  662.7 1.3 copy.44
  664.0 25.7 %select_reduce_fusion.3 = f32[1856,256]{1,0:T(8,128)S(1)} fusion(f32[1856,32]{1,0:T(8,128)S(1)} %bitcast.20, f32[256]{0:T(256)S(1)} %iota_convert_fusion.3, f32[1856,32]{1,0:T(8,128)} %bitcast.21), kind=kLoop, calls=%fused_computation.2.clone.1 | loop fusion | flops 45137920 | bytes 2376704 | tf_op jit(solution)/shard_map/while/body/eval_jaxpr/reduce_sum | solution.py:74
  689.6 3.0 select_add_fusion.2
  692.7 5.5 fusion.4
  698.1 10.8 %multiply_convert_fusion = (bf16[64,1856]{1,0:T(8,128)(2,1)}, bf16[64,1856]{1,0:T(8,128)(2,1)}) fusion(bf16[64,1856]{1,0:T(8,128)(2,1)S(1)} %copy-done.8, bf16[64,1856]{1,0:T(8,128)(2,1)S(1)} %copy-done.9, bf16[64,4096]{1,0:T(8,128)(2,1)S(1)} %copy-done.4, bf16[1856,4096]{1,0:T(8,128)(2,1)} %all-gather.2.cloned.1.call-done), kind=kOutput, calls=%fused_computation.36 | convolution fusion | flops 974860288 | bytes 16678912 | tf_op jit(solution)/shard_map/dot_general | solution.py:31
  (64 shorter events, 13.2 us)
Async XLA Ops:
  7.2 0.9 copy-start.5
  7.2 691.0 %all-gather.2.cloned.1.call-start = ((), (), s32[]{:S(2)}) async-start(), calls=%async_computation | async-start | bytes 19005440 | tf_op jit(solution)/shard_map/all_gather | solution.py:33
  9.4 1.4 copy-start.10
  9.4 12.8 %copy-start.6 = (f32[1,1856,256]{2,1,0:T(8,128)S(1)}, f32[1,1856,256]{2,1,0:T(8,128)}, u32[]{:S(2)}) copy-start(f32[1,1856,256]{2,1,0:T(8,128)} %param.13) | copy-start | bytes 5701636
  10.8 13.3 %copy-start.15 = (f32[256]{0:T(256)}, f32[256]{0:T(256)S(1)}, u32[]{:S(2)}) copy-start(f32[256]{0:T(256)S(1)} %iota_convert_fusion.1) | copy-start | bytes 3076
  10.8 13.3 %copy-start.11 = (f32[256]{0:T(256)}, f32[256]{0:T(256)S(1)}, u32[]{:S(2)}) copy-start(f32[256]{0:T(256)S(1)} %get-tuple-element.69) | copy-start | bytes 3076
  10.8 13.3 %copy-start.13 = (f32[256]{0:T(256)}, f32[256]{0:T(256)S(1)}, u32[]{:S(2)}) copy-start(f32[256]{0:T(256)S(1)} %get-tuple-element.70) | copy-start | bytes 3076
  22.1 1.9 copy-start.3
  24.0 1.3 copy-start
  495.9 0.7 copy-start.17
  495.9 1.2 copy-start.2
  500.2 20.6 %copy-start.1 = (f32[1856,256]{1,0:T(8,128)S(1)}, f32[1856,256]{1,0:T(8,128)}, u32[]{:S(2)}) copy-start(f32[1856,256]{1,0:T(8,128)} %copy-done) | copy-start | bytes 5701636
  500.2 20.6 %copy-start.12 = (f32[256]{0:T(256)S(1)}, f32[256]{0:T(256)}, u32[]{:S(2)}) copy-start(f32[256]{0:T(256)} %copy-done.11) | copy-start | bytes 3076
  500.2 20.6 %copy-start.14 = (f32[256]{0:T(256)S(1)}, f32[256]{0:T(256)}, u32[]{:S(2)}) copy-start(f32[256]{0:T(256)} %copy-done.13) | copy-start | bytes 3076
  500.2 20.6 %copy-start.16 = (f32[256]{0:T(256)S(1)}, f32[256]{0:T(256)}, u32[]{:S(2)}) copy-start(f32[256]{0:T(256)} %copy-done.15) | copy-start | bytes 3076
  520.8 3.9 copy-start.7
  692.7 5.5 copy-start.4
  692.7 5.5 copy-start.8
  692.7 5.5 copy-start.9
Sparse Core Ops, SparseCore 0:
  9.6 263.7 all-gather.1
where the time goes:
time: 717 us; the launch traced here: 716 us
  local copies, waits for them, and re-layouts  485 us (68%)
  other arithmetic  136 us (19%)
  blocking collectives  55.2 us (8%)
  matrix products  24.7 us (3%)
  between operations  14.3 us (2%)
    gather x5, local copies, waits for them, and re-layouts, per_device(): picked = jnp.take_along_axis(spectrum, slot_list, axis=1)  469 us
    reduce_sum x4, other arithmetic, one_worker(): jnp.sum(jnp.where(matches, worker_values[:, :, None], 0.0), axis=1)  103 us
    all_gather x1, blocking collectives, per_device(): lax.all_gather(slot_list.astype(jnp.float32)[None], 'dp', axis=0, tiled=T...  22.4 us
    all_gather x1, blocking collectives, per_device(): lax.all_gather(band_values[None], 'dp', axis=0, tiled=True)  21.5 us
    reduce_sum x1, other arithmetic, per_device(): jnp.sum(jnp.where(slot_list[:, :, None] == frequency[None, None, :], band...  20.6 us
  transfers between devices with their start and end apart: 1, of which 0 were waited for; matrix products, arithmetic and copies ran while one was open for 88% of the time, Pallas kernels for 0%

commit v1 on v0

v1 whole, which is shorter than its diff:
```python
import math

import jax
import jax.numpy as jnp
from jax import lax
from jax.sharding import PartitionSpec as P

momentum_decay = 0.9


def cosine_matrix(length):
    frequency = jnp.arange(length, dtype=jnp.int32).astype(jnp.float32)[:, None]
    position = jnp.arange(length, dtype=jnp.int32).astype(jnp.float32)[None, :]
    angles = math.pi * (position + 0.5) * frequency / length
    row_weight = jnp.where(frequency == 0.0, math.sqrt(1.0 / length), math.sqrt(2.0 / length))
    return jnp.cos(angles) * row_weight


def band_mask(slot_list, counts, length):
    slots = slot_list.T
    slot_ids = jnp.arange(slots.shape[0], dtype=jnp.int32)
    bits = jnp.where(slot_ids[:, None] < counts[None, :], jnp.left_shift(1, slots & 7), 0)
    groups = length // 8
    group = jnp.arange(groups, dtype=jnp.int32)
    group_bytes = jnp.sum(
        jnp.where((slots >> 3)[None, :, :] == group[:, None, None], bits[None, :, :], 0), axis=1
    )
    frequency = jnp.arange(length, dtype=jnp.int32)
    spread = ((frequency >> 3)[None, :] == group[:, None]).astype(jnp.bfloat16)
    expanded = lax.dot_general(
        group_bytes.astype(jnp.bfloat16),
        spread,
        (((0,), (0,)), ((), ())),
        preferred_element_type=jnp.float32,
    )
    return ((expanded.astype(jnp.int32) >> (frequency & 7)[None, :]) & 1) == 1


def per_device(out_grad, gate_pre, up_pre, down_weight, momentum, band_index, band_count):
    worker_rows = gate_pre.shape[0]
    own_rows = gate_pre.shape[1]
    window = momentum.shape[2]
    workers = lax.axis_size("dp")
    block_count = band_index.shape[1]
    length = own_rows * window // block_count
    features = down_weight.shape[1]
    token_rows = out_grad.shape[0]

    window_grad = lax.all_gather(out_grad[:, :window], "fsdp", axis=0, tiled=True)
    by_worker = lax.all_to_all(
        out_grad.reshape(token_rows, workers, features).transpose(1, 0, 2),
        "dp",
        split_axis=0,
        concat_axis=0,
        tiled=True,
    )
    all_grad = lax.all_gather(by_worker, "fsdp", axis=1, tiled=True)
    partial_grad = lax.dot_general(
        all_grad.reshape(workers * worker_rows, features),
        down_weight,
        (((1,), (1,)), ((), ())),
        preferred_element_type=jnp.float32,
    )
    hidden_grad = lax.psum_scatter(partial_grad, "dp", scatter_dimension=0, tiled=True)

    gate_float = gate_pre.astype(jnp.float32)
    up_float = up_pre.astype(jnp.float32)
    sigmoid_gate = jax.nn.sigmoid(gate_float)
    activation = gate_float * sigmoid_gate
    hidden = (activation * up_float).astype(jnp.bfloat16)
    up_grad = (hidden_grad * activation).astype(jnp.bfloat16)
    gate_grad = (
        hidden_grad * up_float * sigmoid_gate * (1.0 + gate_float * (1.0 - sigmoid_gate))
    ).astype(jnp.bfloat16)

    grad_scale = 1.0 / math.sqrt(worker_rows)
    worker_grad = (
        lax.dot_general(
            hidden, window_grad, (((0,), (0,)), ((), ())), preferred_element_type=jnp.float32
        )
        * grad_scale
    )
    cosine_table = cosine_matrix(length)
    momentum_mixed = momentum_decay * momentum[0] + worker_grad
    blocked = momentum_mixed.reshape(block_count, length)
    spectrum = jnp.dot(blocked, cosine_table.T, precision=lax.Precision.HIGHEST)
    own_spectrum = jnp.where(band_mask(band_index[0], band_count[0], length), spectrum, 0.0)
    total = lax.psum_scatter(own_spectrum, "dp", scatter_dimension=0, tiled=True)
    momentum_kept = blocked - jnp.dot(
        own_spectrum, cosine_table, precision=lax.Precision.HIGHEST
    )
    part = jnp.dot(total / workers, cosine_table, precision=lax.Precision.HIGHEST)
    update = lax.all_gather(part, "dp", axis=0, tiled=True)
    return (
        gate_grad,
        up_grad,
        momentum_kept.reshape(1, own_rows, window),
        update.reshape(own_rows, window),
    )


def solution(mesh):
    placed = (
        P(("dp", "fsdp"), None),
        P("dp", "fsdp"),
        P("dp", "fsdp"),
        P("fsdp", "dp"),
        P("dp", "fsdp", None),
        P("dp", "fsdp", None),
        P("dp", "fsdp"),
    )
    return jax.shard_map(
        per_device,
        mesh=mesh,
        in_specs=placed,
        out_specs=(P("dp", "fsdp"), P("dp", "fsdp"), P("dp", "fsdp", None), P("fsdp", None)),
        check_vma=False,
    )
```

time: 717 us -> 167 us (0.23)
  local copies, waits for them, and re-layouts: 485 us -> 5.23 us
  other arithmetic: 136 us -> 5.91 us
  waiting for transfers between devices: 0.68 us -> 89.9 us
  blocking collectives: 55.2 us -> 32.3 us
    gather x5 -> x0, local copies, waits for them, and re-layouts: 469 us -> none  [per_device(): picked = jnp.take_along_axis(spectrum, slot_list, axis=1)]
    reduce_sum x5 -> x1, other arithmetic: 123 us -> 1.17 us  [band_mask(): jnp.sum(jnp.where((slots >> 3)[None, :, :] == group[:, None, None], bits[...]
    reduce_scatter x0 -> x2, waiting for transfers between devices: none -> 48.5 us  [the longest x1 33.9 us: per_device(): lax.psum_scatter(partial_grad, 'dp', scatter_dimension=0, tiled=True)]
    all_gather x1, waiting for transfers between devices: 0.01 us -> 41.4 us  [per_device(): update = lax.all_gather(part, 'dp', axis=0, tiled=True)]
    all_gather x3 -> x2, blocking collectives: 55.2 us -> 20.3 us  [the longest x1 10.5 us: per_device(): lax.all_gather(out_grad[:, :window], 'fsdp', axis=0, tiled=True)]
    all_to_all x0 -> x1, blocking collectives: none -> 12 us  [per_device(): lax.all_to_all(out_grad.reshape(token_rows, workers, features).transpose(...]
    dynamic_slice x12 -> x0, local copies, waits for them, and re-layouts: 10.7 us -> none  [per_device(): lax.scan(one_worker, running, (lax.all_gather(band_values[None], 'dp', ax...]
    add x4 -> x0, other arithmetic: 10.6 us -> none  [one_worker(): partial_sum + jnp.sum(jnp.where(matches, worker_values[:, :, None], 0.0),...]
  transfers between devices with their start and end apart: 1 -> 3, of which waited for: 0 -> 3; matrix products, arithmetic and copies ran while one was open for 88% -> 9% of each run, Pallas kernels for 0% -> 0%
where the time goes in v1:
time: 167 us; the launch traced here: 166 us
  waiting for transfers between devices  89.9 us (54%)
  blocking collectives  32.3 us (19%)
  matrix products  18.5 us (11%)
  between operations  13.8 us (8%)
  other arithmetic  5.91 us (4%)
  local copies, waits for them, and re-layouts  5.23 us (3%)
    all_gather x1, waiting for transfers between devices, per_device(): update = lax.all_gather(part, 'dp', axis=0, tiled=True)  41.4 us
    reduce_scatter x1, waiting for transfers between devices, per_device(): lax.psum_scatter(partial_grad, 'dp', scatter_dimension=0, tiled=True)  33.9 us
    reduce_scatter x1, waiting for transfers between devices, per_device(): lax.psum_scatter(own_spectrum, 'dp', scatter_dimension=0, tiled=True)  14.5 us
    all_to_all x1, blocking collectives, per_device(): lax.all_to_all(out_grad.reshape(token_rows, workers, features).transpose(...  12 us
    all_gather x1, blocking collectives, per_device(): lax.all_gather(out_grad[:, :window], 'fsdp', axis=0, tiled=True)  10.5 us
    all_gather x1, blocking collectives, per_device(): all_grad = lax.all_gather(by_worker, 'fsdp', axis=1, tiled=True)  9.82 us
    dot_general x1, matrix products, per_device(): jnp.dot(own_spectrum, cosine_table, precision=lax.Precision.HIGHEST)  5.45 us
    dot_general x1, matrix products, per_device(): lax.dot_general(all_grad.reshape(workers * worker_rows, features), down_w...  4.69 us
  transfers between devices with their start and end apart: 3, of which 3 were waited for; matrix products, arithmetic and copies ran while one was open for 9% of the time, Pallas kernels for 0%

profile of v1, /device:TPU:0, one launch (start us, length us, event | category | flops | bytes accessed | tf_op | source)
XLA Modules:
  0.0 165.9 jit_solution(13893386100402650302)
XLA Ops:
  7.2 0.7 slice.3
  7.9 10.5 %all_gather.10 = bf16[64,256]{1,0:T(8,128)(2,1)S(1)} all-gather(bf16[8,256]{1,0:T(8,128)(2,1)S(1)} %slice.3), channel_id=1, replica_groups=mesh['dp'=4,'fsdp'=8] {'fsdp'}, dimensions={0}, use_global_device_ids=true | all-gather | bytes 36864 | tf_op jit(solution)/shard_map/all_gather | solution.py:49
  18.4 1.0 shift-right-arithmetic_bitcast_fusion
  19.4 0.7 reduce
  20.1 1.0 bitcast_select_fusion
  21.1 1.2 select_reduce_fusion
  22.3 0.7 fusion.4
  23.0 0.8 copy-done
  23.8 0.1 copy-done.2
  23.9 0.5 fusion
  24.4 3.9 %convolution_select_fusion = f32[1856,256]{1,0:T(8,128)} fusion(pred[1856,256]{1,0:T(32,128)(4,1)S(1)} %fusion.4, f32[1856,256]{1,0:T(8,128)S(1)} %fusion, f32[256]{0:T(256)S(1)} %get-tuple-element.8, f32[256]{0:T(256)S(1)} %iota_convert_fusion, f32[256]{0:T(256)S(1)} %get-tuple-element.9), kind=kOutput, calls=%fused_computation.2 | convolution fusion | flops 1460289536 | bytes 4279296 | tf_op jit(solution)/shard_map/dot_general | solution.py:86
  28.3 0.0 reduce-scatter.3.cloned.1.call-start
  28.3 0.8 copy-done.3
  29.1 12.0 %all_to_all.5 = bf16[4,8,1024]{2,1,0:T(8,128)(2,1)S(1)} all-to-all(bf16[4,8,1024]{2,1,0:T(8,128)(2,1)S(1)} %bitcast.22), channel_id=1, replica_groups=mesh['dp'=4,'fsdp'=8] {'dp'}, dimensions={0} | all-to-all | bytes 131072 | tf_op jit(solution)/shard_map/all_to_all | solution.py:50
  41.1 9.8 %all_gather.9 = bf16[4,64,1024]{2,1,0:T(8,128)(2,1)S(1)} all-gather(bf16[4,8,1024]{2,1,0:T(8,128)(2,1)S(1)} %all_to_all.5), channel_id=1, replica_groups=mesh['dp'=4,'fsdp'=8] {'fsdp'}, dimensions={1}, use_global_device_ids=true | all-gather | bytes 589824 | tf_op jit(solution)/shard_map/all_gather | solution.py:57
  50.9 4.7 %fusion.36 = f32[256,1856]{1,0:T(8,128)} fusion(bf16[256,1024]{1,0:T(8,128)(2,1)S(1)} %bitcast.21, bf16[1856,1024]{1,0:T(8,128)(2,1)} %param.10), kind=kOutput, calls=%fused_computation.57 | convolution fusion | flops 973078528 | bytes 6225920 | tf_op jit(solution)/shard_map/dot_general | solution.py:58
  55.6 0.2 all-gather.2.cloned.1.call-start
  55.8 14.5 %reduce-scatter.5.cloned.1.call-done = f32[464,256]{1,0:T(8,128)} async-done(((f32[1856,256]{1,0:T(8,128)}), f32[464,256]{1,0:T(8,128)}) %reduce-scatter.5.cloned.1.call-update) | async-done | bytes 475152 | tf_op jit(solution)/shard_map/reduce_scatter | solution.py:88
  70.3 3.3 %fusion.13 = f32[464,256]{1,0:T(8,128)} fusion(f32[464,256]{1,0:T(8,128)} %reduce-scatter.5.cloned.1.call-done, f32[256]{0:T(256)S(1)} %get-tuple-element.8, f32[256]{0:T(256)S(1)} %iota_convert_fusion, f32[256]{0:T(256)S(1)} %get-tuple-element.9), kind=kOutput, calls=%fused_computation.25 | convolution fusion | flops 365219840 | bytes 953344 | tf_op jit(solution)/shard_map/dot_general | solution.py:92
  73.7 5.4 %fusion.1 = f32[1,1856,256]{2,1,0:T(8,128)} fusion(f32[1856,256]{1,0:T(8,128)S(1)} %fusion, f32[1856,256]{1,0:T(8,128)} %convolution_select_fusion, f32[256]{0:T(256)S(1)} %get-tuple-element.8, f32[256]{0:T(256)S(1)} %iota_convert_fusion, f32[256]{0:T(256)S(1)} %get-tuple-element.9), kind=kOutput, calls=%fused_computation.6 | convolution fusion | flops 1460289536 | bytes 5704704 | tf_op jit(solution)/shard_map/dot_general | solution.py:89
  79.1 33.9 %reduce-scatter.3.cloned.1.call-done = f32[64,1856]{1,0:T(8,128)} async-done(((f32[256,1856]{1,0:T(8,128)}), f32[64,1856]{1,0:T(8,128)}) %reduce-scatter.3.cloned.1.call-update) | async-done | bytes 475152 | tf_op jit(solution)/shard_map/reduce_scatter | solution.py:64
  113.1 2.1 %multiply_convert_fusion = (bf16[64,1856]{1,0:T(8,128)(2,1)}, bf16[64,1856]{1,0:T(8,128)(2,1)}) fusion(f32[64,1856]{1,0:T(8,128)} %reduce-scatter.3.cloned.1.call-done, bf16[64,1856]{1,0:T(8,128)(2,1)S(1)} %copy-done.2, bf16[64,1856]{1,0:T(8,128)(2,1)S(1)} %copy-done.1), kind=kLoop, calls=%fused_computation.24 | loop fusion | flops 1781760 | bytes 1425408 | tf_op jit(solution)/shard_map/convert_element_type | solution.py:71
  115.1 41.4 %all-gather.2.cloned.1.call-done = f32[1856,256]{1,0:T(8,128)} async-done(((f32[464,256]{1,0:T(8,128)}), f32[1856,256]{1,0:T(8,128)}) %all-gather.2.cloned.1.call-update) | async-done | bytes 1900560 | tf_op jit(solution)/shard_map/all_gather | solution.py:93
  156.5 2.9 %copy.14 = f32[1856,256]{1,0:T(8,128)} copy(f32[1856,256]{1,0:T(8,128)} %all-gather.2.cloned.1.call-done) | data formatting | bytes 3801088
  (12 shorter events, 0.1 us)
Async XLA Ops:
  7.2 63.2 %reduce-scatter.5.cloned.1.call-start = ((), (), s32[]{:S(2)}) async-start(), calls=%async_computation.4 | async-start | bytes 2375680 | tf_op jit(solution)/shard_map/reduce_scatter | solution.py:88
  22.3 1.5 copy-start
  22.3 1.5 copy-start.1
  22.3 1.6 copy-start.2
  28.2 0.8 copy-start.3
  28.3 84.8 %reduce-scatter.3.cloned.1.call-start = ((), (), s32[]{:S(2)}) async-start(), calls=%async_computation.3 | async-start | bytes 2457600 | tf_op jit(solution)/shard_map/reduce_scatter | solution.py:64
  55.6 100.9 %all-gather.2.cloned.1.call-start = ((), (), s32[]{:S(2)}) async-start(), calls=%async_computation.5 | async-start | bytes 2375680 | tf_op jit(solution)/shard_map/all_gather | solution.py:93
Sparse Core Ops, SparseCore 0:
  28.4 41.9 reduce-scatter.4
  72.8 40.2 reduce-scatter.2
  114.7 41.7 all-gather.1

commit v2 on v1

--- a/solution.py
+++ b/solution.py
@@ -3,6 +3,8 @@
 import jax
 import jax.numpy as jnp
 from jax import lax
+from jax.experimental import pallas as pl
+from jax.experimental.pallas import tpu as pltpu
 from jax.sharding import PartitionSpec as P
 
 momentum_decay = 0.9
@@ -16,24 +18,134 @@
     return jnp.cos(angles) * row_weight
 
 
-def band_mask(slot_list, counts, length):
+lanes = 128
+
+
+def sorted_slots(slot_list, counts, length):
     slots = slot_list.T
     slot_ids = jnp.arange(slots.shape[0], dtype=jnp.int32)
-    bits = jnp.where(slot_ids[:, None] < counts[None, :], jnp.left_shift(1, slots & 7), 0)
-    groups = length // 8
-    group = jnp.arange(groups, dtype=jnp.int32)
-    group_bytes = jnp.sum(
-        jnp.where((slots >> 3)[None, :, :] == group[:, None, None], bits[None, :, :], 0), axis=1
-    )
+    keys = jnp.where(slot_ids[:, None] < counts[None, :], slots, length + slot_ids[:, None])
+    rank = jnp.sum((keys[:, None, :] < keys[None, :, :]).astype(jnp.int32), axis=0)
+    ordered = jnp.sum(
+        jnp.where(rank[:, None, :] == slot_ids[None, :, None], keys[:, None, :], 0), axis=0
+    )
+    return jnp.minimum(ordered, length)
+
+
+def group_bytes(slots, length):
+    group = jnp.arange(length // 8, dtype=jnp.int32)
+    bits = jnp.left_shift(1, slots & 7)
+    return jnp.sum(
+        jnp.where(
+            (slots >> 3)[..., None, :, :] == group[:, None, None], bits[..., None, :, :], 0
+        ),
+        axis=-2,
+    ).astype(jnp.bfloat16)
+
+
+def spread_matrix(length):
+    group = jnp.arange(length // 8, dtype=jnp.int32)
     frequency = jnp.arange(length, dtype=jnp.int32)
-    spread = ((frequency >> 3)[None, :] == group[:, None]).astype(jnp.bfloat16)
-    expanded = lax.dot_general(
-        group_bytes.astype(jnp.bfloat16),
-        spread,
-        (((0,), (0,)), ((), ())),
+    return ((frequency >> 3)[None, :] == group[:, None]).astype(jnp.bfloat16)
+
+
+def below_matrix(length):
+    frequency = jnp.arange(length, dtype=jnp.int32)
+    return (frequency[:, None] < frequency[None, :]).astype(jnp.bfloat16)
+
+
+def lane_pick(values, places):
+    return jnp.take_along_axis(values, places, axis=1, mode="promise_in_bounds")
+
+
+def tile_rows(rows):
+    return rows // 4 if rows % 64 == 0 else rows
+
+
+def pick_kernel(spectrum_ref, places_ref, picked_ref):
+    places = places_ref[...]
+    inside = places & (lanes - 1)
+    picked = jnp.zeros(places.shape, jnp.float32)
+    for start in range(0, spectrum_ref.shape[1], lanes):
+        here = lane_pick(spectrum_ref[:, start : start + lanes], inside)
+        picked = jnp.where((places >= start) & (places < start + lanes), here, picked)
+    picked_ref[...] = picked
+
+
+def pick(spectrum, places):
+    rows, length = spectrum.shape
+    tile = tile_rows(rows)
+    return pl.pallas_call(
+        pick_kernel,
+        grid=(rows // tile,),
+        out_shape=jax.ShapeDtypeStruct((rows, lanes), jnp.float32),
+        in_specs=[
+            pl.BlockSpec((tile, length), lambda i: (i, 0)),
+            pl.BlockSpec((tile, lanes), lambda i: (i, 0)),
+        ],
+        out_specs=pl.BlockSpec((tile, lanes), lambda i: (i, 0)),
+        compiler_params=pltpu.CompilerParams(vmem_limit_bytes=24 * 2**20),
+        cost_estimate=pl.CostEstimate(
+            flops=rows * length * 4, bytes_accessed=rows * length * 8, transcendentals=0
+        ),
+    )(spectrum, places)
+
+
+def update_kernel(values_ref, bytes_ref, spread_ref, below_ref, table_ref, update_ref):
+    workers, tile = values_ref.shape[0], values_ref.shape[1]
+    length = table_ref.shape[0]
+    shift = lax.broadcasted_iota(jnp.int32, (tile, length), 1) & 7
+    total = [jnp.zeros((tile, lanes), jnp.float32) for _ in range(length // lanes)]
+    for worker in range(workers):
+        expanded = jnp.dot(
+            bytes_ref[worker], spread_ref[...], preferred_element_type=jnp.float32
+        ).astype(jnp.int32)
+        used = (expanded >> shift) & 1
+        rank = jnp.dot(
+            used.astype(jnp.float32).astype(jnp.bfloat16),
+            below_ref[...],
+            preferred_element_type=jnp.float32,
+        ).astype(jnp.int32)
+        values = values_ref[worker]
+        values = jnp.concatenate(
+            [values, jnp.zeros((tile, lanes - values.shape[1]), jnp.float32)], axis=1
+        )
+        for part in range(length // lanes):
+            columns = slice(part * lanes, (part + 1) * lanes)
+            here = lane_pick(values, rank[:, columns] & (lanes - 1))
+            total[part] = total[part] + jnp.where(used[:, columns] == 1, here, 0.0)
+    averaged = jnp.concatenate(total, axis=1) * (1.0 / workers)
+    update_ref[...] = jnp.dot(
+        averaged,
+        table_ref[...],
+        precision=lax.Precision.HIGHEST,
         preferred_element_type=jnp.float32,
     )
-    return ((expanded.astype(jnp.int32) >> (frequency & 7)[None, :]) & 1) == 1
+
+
+def summed_update(values, group_rows, table):
+    workers, rows, slot_count = values.shape
+    length = table.shape[0]
+    groups = group_rows.shape[2]
+    tile = tile_rows(rows)
+    whole = lambda i: (0, 0)
+    return pl.pallas_call(
+        update_kernel,
+        grid=(rows // tile,),
+        out_shape=jax.ShapeDtypeStruct((rows, length), jnp.float32),
+        in_specs=[
+            pl.BlockSpec((workers, tile, slot_count), lambda i: (0, i, 0)),
+            pl.BlockSpec((workers, tile, groups), lambda i: (0, i, 0)),
+            pl.BlockSpec((groups, length), whole),
+            pl.BlockSpec((length, length), whole),
+            pl.BlockSpec((length, length), whole),
+        ],
+        out_specs=pl.BlockSpec((tile, length), lambda i: (i, 0)),
+        compiler_params=pltpu.CompilerParams(vmem_limit_bytes=40 * 2**20),
+        cost_estimate=pl.CostEstimate(
+            flops=rows * length * length * 16, bytes_accessed=rows * length * 16, transcendentals=0
+        ),
+    )(values, group_rows, spread_matrix(length), below_matrix(length), table)
 
 
 def per_device(out_grad, gate_pre, up_pre, down_weight, momentum, band_index, band_count):
@@ -46,6 +158,20 @@
     features = down_weight.shape[1]
     token_rows = out_grad.shape[0]
 
+    slots = sorted_slots(band_index[0], band_count[0], length)
+    slot_count = slots.shape[0]
+    all_slots = lax.all_gather(slots.astype(jnp.bfloat16), "dp", axis=0)
+    all_bytes = group_bytes(all_slots.astype(jnp.int32), length).transpose(0, 2, 1)
+    places = jnp.pad(slots.T, ((0, 0), (0, lanes - slot_count)), constant_values=length)
+    frequency = jnp.arange(length, dtype=jnp.int32)
+    expanded = lax.dot_general(
+        group_bytes(slots, length),
+        spread_matrix(length),
+        (((0,), (0,)), ((), ())),
+        preferred_element_type=jnp.float32,
+    )
+    mask = ((expanded.astype(jnp.int32) >> (frequency & 7)[None, :]) & 1) == 1
+
     window_grad = lax.all_gather(out_grad[:, :window], "fsdp", axis=0, tiled=True)
     by_worker = lax.all_to_all(
         out_grad.reshape(token_rows, workers, features).transpose(1, 0, 2),
@@ -84,13 +210,13 @@
     momentum_mixed = momentum_decay * momentum[0] + worker_grad
     blocked = momentum_mixed.reshape(block_count, length)
     spectrum = jnp.dot(blocked, cosine_table.T, precision=lax.Precision.HIGHEST)
-    own_spectrum = jnp.where(band_mask(band_index[0], band_count[0], length), spectrum, 0.0)
-    total = lax.psum_scatter(own_spectrum, "dp", scatter_dimension=0, tiled=True)
+    picked = pick(spectrum, places)[:, :slot_count].T
+    all_values = lax.all_gather(picked, "dp", axis=0)
+    own_spectrum = jnp.where(mask, spectrum, 0.0)
     momentum_kept = blocked - jnp.dot(
         own_spectrum, cosine_table, precision=lax.Precision.HIGHEST
     )
-    part = jnp.dot(total / workers, cosine_table, precision=lax.Precision.HIGHEST)
-    update = lax.all_gather(part, "dp", axis=0, tiled=True)
+    update = summed_update(all_values.transpose(0, 2, 1), all_bytes, cosine_table)
     return (
         gate_grad,
         up_grad,

time: 167 us -> 153 us (0.916)
  waiting for transfers between devices: 89.9 us -> 0.02 us
  blocking collectives: 32.3 us -> 73.4 us
  local copies, waits for them, and re-layouts: 5.23 us -> 17.6 us
  Pallas kernels: 0 us -> 12.3 us
  other arithmetic: 5.91 us -> 16 us
  matrix products: 18.5 us -> 12.2 us
  starting transfers between devices: 0.3 us -> 6.33 us
    all_gather x0 -> x2, blocking collectives: none -> 54.5 us  [the longest x1 32.6 us: per_device(): all_values = lax.all_gather(picked, 'dp', axis=0)]
    all_gather x1 -> x0, waiting for transfers between devices: 41.4 us -> none  [per_device(): update = lax.all_gather(part, 'dp', axis=0, tiled=True)]
    reduce_scatter x1, waiting for transfers between devices: 33.9 us -> 0.01 us  [per_device(): lax.psum_scatter(partial_grad, 'dp', scatter_dimension=0, tiled=True)]
    reduce_scatter x1 -> x0, waiting for transfers between devices: 14.5 us -> none  [per_device(): lax.psum_scatter(own_spectrum, 'dp', scatter_dimension=0, tiled=True)]
    pallas_call x0 -> x2, Pallas kernels: none -> 12.3 us  [the longest x1 10.7 us: summed_update(): pl.pallas_call(update_kernel, grid=(rows // tile,), out_shape=jax.ShapeDt...]
    all_to_all x1 -> x0, blocking collectives: 12 us -> none  [per_device(): lax.all_to_all(out_grad.reshape(token_rows, workers, features).transpose(...]
    reduce_sum x1 -> x4, other arithmetic: 1.17 us -> 9.79 us  [the longest x2 7.67 us: group_bytes(): jnp.sum(jnp.where((slots >> 3)[..., None, :, :] == group[:, None, None],...]
    all_to_all x0 -> x1, starting transfers between devices: none -> 6.33 us  [per_device(): lax.all_to_all(out_grad.reshape(token_rows, workers, features).transpose(...]
  transfers between devices with their start and end apart: 3 -> 2, of which waited for: 3 -> 0; matrix products, arithmetic and copies ran while one was open for 9% -> 21% of each run, Pallas kernels for 0% -> 8%
where the time goes in v2:
time: 153 us; the launch traced here: 152 us
  blocking collectives  73.4 us (48%)
  local copies, waits for them, and re-layouts  17.6 us (12%)
  other arithmetic  16 us (10%)
  between operations  14.2 us (9%)
  Pallas kernels  12.3 us (8%)
  matrix products  12.2 us (8%)
  starting transfers between devices  6.33 us (4%)
    all_gather x1, blocking collectives, per_device(): all_values = lax.all_gather(picked, 'dp', axis=0)  32.6 us
    all_gather x1, blocking collectives, per_device(): all_slots = lax.all_gather(slots.astype(jnp.bfloat16), 'dp', axis=0)  21.9 us
    pallas_call x1, Pallas kernels, summed_update(): pl.pallas_call(update_kernel, grid=(rows // tile,), out_shape=jax.ShapeDt...  10.7 us
    all_gather x1, blocking collectives, per_device(): all_grad = lax.all_gather(by_worker, 'fsdp', axis=1, tiled=True)  9.84 us
    all_gather x1, blocking collectives, per_device(): lax.all_gather(out_grad[:, :window], 'fsdp', axis=0, tiled=True)  9.06 us
    reduce_sum x2, other arithmetic, group_bytes(): jnp.sum(jnp.where((slots >> 3)[..., None, :, :] == group[:, None, None],...  7.67 us
    unnamed x20, local copies, waits for them, and re-layouts  7.24 us
    all_to_all x1, starting transfers between devices, per_device(): lax.all_to_all(out_grad.reshape(token_rows, workers, features).transpose(...  6.33 us
  transfers between devices with their start and end apart: 2, of which 0 were waited for; matrix products, arithmetic and copies ran while one was open for 21% of the time, Pallas kernels for 8%

profile of v2, /device:TPU:0, one launch (start us, length us, event | category | flops | bytes accessed | tf_op | source)
XLA Modules:
  0.0 152.2 jit_solution(6884345400396449699)
XLA Ops:
  7.2 6.3 %all-to-all-start = ((bf16[4,8,1024]{2,1,0:T(8,128)(2,1)}), bf16[4,8,1024]{2,1,0:T(8,128)(2,1)}, u32[]{:S(2)}, u32[]{:S(2)}) async-start(bf16[4,8,1024]{2,1,0:T(8,128)(2,1)} %bitcast.32), calls=%async_computation | async-start | bytes 131072 | tf_op jit(solution)/shard_map/all_to_all | solution.py:176
  14.2 9.1 %all_gather.17 = bf16[64,256]{1,0:T(8,128)(2,1)S(1)} all-gather(bf16[8,256]{1,0:T(8,128)(2,1)S(1)} %slice.6), channel_id=1, replica_groups=mesh['dp'=4,'fsdp'=8] {'fsdp'}, dimensions={0}, use_global_device_ids=true | all-gather | bytes 36864 | tf_op jit(solution)/shard_map/all_gather | solution.py:175
  24.0 1.0 bitcast_select_fusion
  25.8 1.3 select_reduce_fusion.2
  27.5 1.2 minimum_convert_fusion
  28.8 1.4 copy-done.4
  30.7 1.2 copy-done.2
  31.9 2.6 %fusion.17.spectrum_ref = f32[1856,256]{1,0:T(8,128)S(1)} fusion(f32[1856,256]{1,0:T(8,128)S(1)} %fusion, f32[256]{0:T(256)S(1)} %get-tuple-element.12, f32[256]{0:T(256)S(1)} %iota_convert_fusion, f32[256]{0:T(256)S(1)} %get-tuple-element.13), kind=kOutput, calls=%fused_computation.43 | convolution fusion | flops 1459814400 | bytes 3804160 | tf_op jit(solution)/shard_map/dot_general | solution.py:212
  34.6 1.6 %shard_map.102 = f32[1856,128]{1,0:T(8,128)S(1)} custom-call(f32[1856,256]{1,0:T(8,128)S(1)} %fusion.17.spectrum_ref, s32[1856,128]{1,0:T(8,128)S(1)} %pad.4.places_ref), custom_call_target="tpu_custom_call" | custom-call | flops 1900544 | bytes 3801088 | tf_op jit(solution)/shard_map/pallas_call | solution.py:78
  37.4 1.5 copy.36
  39.9 1.5 copy.37
  41.4 9.8 %all_gather.16 = bf16[4,64,1024]{2,1,0:T(8,128)(2,1)S(1)} all-gather(bf16[4,8,1024]{2,1,0:T(8,128)(2,1)} %all-to-all-done), channel_id=1, replica_groups=mesh['dp'=4,'fsdp'=8] {'fsdp'}, dimensions={1}, use_global_device_ids=true | all-gather | bytes 589824 | tf_op jit(solution)/shard_map/all_gather | solution.py:183
  51.2 4.7 %fusion.32 = f32[256,1856]{1,0:T(8,128)} fusion(bf16[256,1024]{1,0:T(8,128)(2,1)S(1)} %bitcast.31, bf16[1856,1024]{1,0:T(8,128)(2,1)} %param.10), kind=kOutput, calls=%fused_computation.65 | convolution fusion | flops 973078528 | bytes 6225920 | tf_op jit(solution)/shard_map/dot_general | solution.py:184
  56.0 21.9 %all-gather.1 = bf16[128,1856]{1,0:T(8,128)(2,1)S(1)} all-gather(bf16[32,1856]{1,0:T(8,128)(2,1)S(1)} %copy.39), channel_id=3, replica_groups=mesh['dp'=4,'fsdp'=8] {'dp'}, dimensions={0}, use_global_device_ids=true | all-gather | bytes 593920 | tf_op jit(solution)/shard_map/all_gather | solution.py:163
  78.1 6.5 %select_reduce_fusion = s32[4,32,1856]{2,1,0:T(8,128)S(1)} fusion(s32[4,32,1856]{2,1,0:T(8,128)S(1)} %bitcast.30, s32[4,32,1856]{2,1,0:T(8,128)S(1)} %bitcast.29), kind=kLoop, calls=%fused_computation | loop fusion | flops 22568960 | bytes 2850816 | tf_op jit(solution)/shard_map/reduce_sum | solution.py:38
  84.6 1.7 %copy.40 = bf16[4,32,1856]{1,2,0:T(8,128)(2,1)} copy(bf16[4,32,1856]{2,1,0:T(8,128)(2,1)S(1)} %convert_element_type.85) | data formatting | bytes 950272 | tf_op jit(solution)/shard_map/convert_element_type | solution.py:43
  86.3 32.6 %all-gather = f32[128,1856]{1,0:T(8,128)S(1)} all-gather(f32[32,1856]{1,0:T(8,128)S(1)} %copy.37), channel_id=2, replica_groups=mesh['dp'=4,'fsdp'=8] {'dp'}, dimensions={0}, use_global_device_ids=true | all-gather | bytes 1187840 | tf_op jit(solution)/shard_map/all_gather | solution.py:214
  118.9 2.5 %copy.38 = f32[4,32,1856]{1,2,0:T(8,128)} copy(f32[4,32,1856]{2,1,0:T(8,128)S(1)} %bitcast.28) | data formatting | bytes 1900544 | tf_op jit(solution)/shard_map/all_gather | solution.py:214
  122.4 2.1 %copy-done = f32[4,32,1856]{1,2,0:T(8,128)S(1)} copy-done((f32[4,32,1856]{1,2,0:T(8,128)S(1)}, f32[4,32,1856]{1,2,0:T(8,128)}, u32[]{:S(2)}) %copy-start) | copy-done | bytes 950296
  124.4 1.5 copy-done.1
  126.0 10.7 %shard_map.103 = f32[1856,256]{1,0:T(8,128)} custom-call(f32[4,1856,32]{2,1,0:T(8,128)S(1)} %bitcast.26, bf16[4,1856,32]{2,1,0:T(8,128)(2,1)S(1)} %bitcast.27, bf16[32,256]{1,0:T(8,128)(2,1)S(1)} %fusion.27.spread_ref, bf16[256,256]{1,0:T(8,128)(2,1)S(1)} %fusion.15.below_ref, f32[256,256]{1,0:T(8,128)S(1)} %cosine_multiply_fusion.table_ref), custom_call_target="tpu_custom_call" | custom-call | flops 1946157056 | bytes 7602176 | tf_op jit(solution)/shard_map/pallas_call | solution.py:132
  136.7 1.2 select_reduce_fusion.1
  139.4 3.9 %fusion.1 = f32[1,1856,256]{2,1,0:T(8,128)} fusion(f32[1856,256]{1,0:T(8,128)S(1)} %copy-done.3, f32[1856,256]{1,0:T(8,128)S(1)} %fusion.5, f32[256]{0:T(256)S(1)} %get-tuple-element.12, f32[256]{0:T(256)S(1)} %iota_convert_fusion, f32[256]{0:T(256)S(1)} %get-tuple-element.13), kind=kOutput, calls=%fused_computation.10 | convolution fusion | flops 1460289536 | bytes 5704704 | tf_op jit(solution)/shard_map/dot_general | solution.py:216
  143.3 2.1 %multiply_convert_fusion = (bf16[64,1856]{1,0:T(8,128)(2,1)}, bf16[64,1856]{1,0:T(8,128)(2,1)}) fusion(f32[64,1856]{1,0:T(8,128)} %reduce-scatter.2.cloned.1.call-done, bf16[64,1856]{1,0:T(8,128)(2,1)S(1)} %copy-done.7, bf16[64,1856]{1,0:T(8,128)(2,1)S(1)} %copy-done.9), kind=kLoop, calls=%fused_computation.37 | loop fusion | flops 1781760 | bytes 1425408 | tf_op jit(solution)/shard_map/convert_element_type | solution.py:197
  (40 shorter events, 8.1 us)
Async XLA Ops:
  7.2 34.2 %all-to-all-start = ((bf16[4,8,1024]{2,1,0:T(8,128)(2,1)}), bf16[4,8,1024]{2,1,0:T(8,128)(2,1)}, u32[]{:S(2)}, u32[]{:S(2)}) async-start(bf16[4,8,1024]{2,1,0:T(8,128)(2,1)} %bitcast.32), calls=%async_computation | async-start | bytes 131072 | tf_op jit(solution)/shard_map/all_to_all | solution.py:176
  13.5 129.8 %reduce-scatter.2.cloned.1.call-start = ((), (), s32[]{:S(2)}) async-start(), calls=%async_computation.2 | async-start | bytes 2457600 | tf_op jit(solution)/shard_map/reduce_scatter | solution.py:190
  27.5 1.3 copy-start.6
  27.5 1.3 copy-start.8
  28.7 1.5 %copy-start.4 = (f32[1,1856,256]{2,1,0:T(8,128)S(1)}, f32[1,1856,256]{2,1,0:T(8,128)}, u32[]{:S(2)}) copy-start(f32[1,1856,256]{2,1,0:T(8,128)} %param.11) | copy-start | bytes 5701636
  30.7 1.3 copy-start.2
  122.4 2.1 %copy-start = (f32[4,32,1856]{1,2,0:T(8,128)S(1)}, f32[4,32,1856]{1,2,0:T(8,128)}, u32[]{:S(2)}) copy-start(f32[4,32,1856]{1,2,0:T(8,128)} %copy.38) | copy-start | bytes 2850820
  124.4 1.5 %copy-start.1 = (bf16[4,32,1856]{1,2,0:T(8,128)(2,1)S(1)}, bf16[4,32,1856]{1,2,0:T(8,128)(2,1)}, u32[]{:S(2)}) copy-start(bf16[4,32,1856]{1,2,0:T(8,128)(2,1)} %copy.40) | copy-start | bytes 1425412
  126.0 10.7 %copy-start.5 = (s32[32,1856]{1,0:T(8,128)S(1)}, s32[32,1856]{1,0:T(8,128)}, u32[]{:S(2)}) copy-start(s32[32,1856]{1,0:T(8,128)} %copy.35) | copy-start | bytes 712708
  137.8 1.5 %copy-start.3 = (f32[1856,256]{1,0:T(8,128)S(1)}, f32[1856,256]{1,0:T(8,128)}, u32[]{:S(2)}) copy-start(f32[1856,256]{1,0:T(8,128)} %copy-done.2) | copy-start | bytes 5701636
  139.4 3.9 %copy-start.7 = (bf16[64,1856]{1,0:T(8,128)(2,1)S(1)}, bf16[64,1856]{1,0:T(8,128)(2,1)}, u32[]{:S(2)}) copy-start(bf16[64,1856]{1,0:T(8,128)(2,1)} %param.8) | copy-start | bytes 712708
  139.4 3.9 %copy-start.9 = (bf16[64,1856]{1,0:T(8,128)(2,1)S(1)}, bf16[64,1856]{1,0:T(8,128)(2,1)}, u32[]{:S(2)}) copy-start(bf16[64,1856]{1,0:T(8,128)(2,1)} %param.9) | copy-start | bytes 712708
Sparse Core Ops, SparseCore 0:
  56.1 58.7 reduce-scatter.1

commit v3 on v2

--- a/solution.py
+++ b/solution.py
@@ -56,6 +56,13 @@
 
 def lane_pick(values, places):
     return jnp.take_along_axis(values, places, axis=1, mode="promise_in_bounds")
+
+
+def from_each(block, workers):
+    return [block] + [
+        lax.ppermute(block, "dp", [(i, (i + step) % workers) for i in range(workers)])
+        for step in range(1, workers)
+    ]
 
 
 def tile_rows(rows):
@@ -91,14 +98,15 @@
     )(spectrum, places)
 
 
-def update_kernel(values_ref, bytes_ref, spread_ref, below_ref, table_ref, update_ref):
+def update_kernel(own_ref, values_ref, bytes_ref, spread_ref, below_ref, table_ref, update_ref):
     workers, tile = values_ref.shape[0], values_ref.shape[1]
     length = table_ref.shape[0]
     shift = lax.broadcasted_iota(jnp.int32, (tile, length), 1) & 7
     total = [jnp.zeros((tile, lanes), jnp.float32) for _ in range(length // lanes)]
     for worker in range(workers):
+        held = lax.rem(own_ref[0] - worker + workers, workers)
         expanded = jnp.dot(
-            bytes_ref[worker], spread_ref[...], preferred_element_type=jnp.float32
+            bytes_ref[held], spread_ref[...], preferred_element_type=jnp.float32
         ).astype(jnp.int32)
         used = (expanded >> shift) & 1
         rank = jnp.dot(
@@ -106,7 +114,7 @@
             below_ref[...],
             preferred_element_type=jnp.float32,
         ).astype(jnp.int32)
-        values = values_ref[worker]
+        values = values_ref[held]
         values = jnp.concatenate(
             [values, jnp.zeros((tile, lanes - values.shape[1]), jnp.float32)], axis=1
         )
@@ -123,7 +131,7 @@
     )
 
 
-def summed_update(values, group_rows, table):
+def summed_update(own, values, group_rows, table):
     workers, rows, slot_count = values.shape
     length = table.shape[0]
     groups = group_rows.shape[2]
@@ -134,6 +142,7 @@
         grid=(rows // tile,),
         out_shape=jax.ShapeDtypeStruct((rows, length), jnp.float32),
         in_specs=[
+            pl.BlockSpec(memory_space=pltpu.SMEM),
             pl.BlockSpec((workers, tile, slot_count), lambda i: (0, i, 0)),
             pl.BlockSpec((workers, tile, groups), lambda i: (0, i, 0)),
             pl.BlockSpec((groups, length), whole),
@@ -145,7 +154,7 @@
         cost_estimate=pl.CostEstimate(
             flops=rows * length * length * 16, bytes_accessed=rows * length * 16, transcendentals=0
         ),
-    )(values, group_rows, spread_matrix(length), below_matrix(length), table)
+    )(own, values, group_rows, spread_matrix(length), below_matrix(length), table)
 
 
 def per_device(out_grad, gate_pre, up_pre, down_weight, momentum, band_index, band_count):
@@ -158,21 +167,6 @@
     features = down_weight.shape[1]
     token_rows = out_grad.shape[0]
 
-    slots = sorted_slots(band_index[0], band_count[0], length)
-    slot_count = slots.shape[0]
-    all_slots = lax.all_gather(slots.astype(jnp.bfloat16), "dp", axis=0)
-    all_bytes = group_bytes(all_slots.astype(jnp.int32), length).transpose(0, 2, 1)
-    places = jnp.pad(slots.T, ((0, 0), (0, lanes - slot_count)), constant_values=length)
-    frequency = jnp.arange(length, dtype=jnp.int32)
-    expanded = lax.dot_general(
-        group_bytes(slots, length),
-        spread_matrix(length),
-        (((0,), (0,)), ((), ())),
-        preferred_element_type=jnp.float32,
-    )
-    mask = ((expanded.astype(jnp.int32) >> (frequency & 7)[None, :]) & 1) == 1
-
-    window_grad = lax.all_gather(out_grad[:, :window], "fsdp", axis=0, tiled=True)
     by_worker = lax.all_to_all(
         out_grad.reshape(token_rows, workers, features).transpose(1, 0, 2),
         "dp",
@@ -180,14 +174,41 @@
         concat_axis=0,
         tiled=True,
     )
-    all_grad = lax.all_gather(by_worker, "fsdp", axis=1, tiled=True)
+    extra = -(-window // features)
+    tail = jnp.pad(out_grad[:, :window], ((0, 0), (0, extra * features - window)))
+    tail = tail.reshape(token_rows, extra, features).transpose(1, 0, 2)
+    gathered = lax.all_gather(
+        jnp.concatenate([by_worker, tail], axis=0), "fsdp", axis=1, tiled=True
+    )
     partial_grad = lax.dot_general(
-        all_grad.reshape(workers * worker_rows, features),
+        gathered[:workers].reshape(workers * worker_rows, features),
         down_weight,
         (((1,), (1,)), ((), ())),
         preferred_element_type=jnp.float32,
     )
+    _, gathered, momentum, band_index, band_count = lax.optimization_barrier(
+        (partial_grad[:1, :1], gathered, momentum, band_index, band_count)
+    )
     hidden_grad = lax.psum_scatter(partial_grad, "dp", scatter_dimension=0, tiled=True)
+    window_grad = jnp.concatenate([gathered[workers + i] for i in range(extra)], axis=1)
+    window_grad = window_grad[:, :window]
+
+    slots = sorted_slots(band_index[0], band_count[0], length)
+    slot_count = slots.shape[0]
+    all_slots = from_each(slots.astype(jnp.bfloat16), workers)
+    own_bytes = group_bytes(slots, length)
+    all_bytes = jnp.stack(
+        [own_bytes] + [group_bytes(got.astype(jnp.int32), length) for got in all_slots[1:]]
+    ).transpose(0, 2, 1)
+    places = jnp.pad(slots.T, ((0, 0), (0, lanes - slot_count)), constant_values=length)
+    frequency = jnp.arange(length, dtype=jnp.int32)
+    expanded = lax.dot_general(
+        own_bytes,
+        spread_matrix(length),
+        (((0,), (0,)), ((), ())),
+        preferred_element_type=jnp.float32,
+    )
+    mask = ((expanded.astype(jnp.int32) >> (frequency & 7)[None, :]) & 1) == 1
 
     gate_float = gate_pre.astype(jnp.float32)
     up_float = up_pre.astype(jnp.float32)
@@ -211,12 +232,13 @@
     blocked = momentum_mixed.reshape(block_count, length)
     spectrum = jnp.dot(blocked, cosine_table.T, precision=lax.Precision.HIGHEST)
     picked = pick(spectrum, places)[:, :slot_count].T
-    all_values = lax.all_gather(picked, "dp", axis=0)
+    all_values = jnp.stack(from_each(picked, workers))
     own_spectrum = jnp.where(mask, spectrum, 0.0)
     momentum_kept = blocked - jnp.dot(
         own_spectrum, cosine_table, precision=lax.Precision.HIGHEST
     )
-    update = summed_update(all_values.transpose(0, 2, 1), all_bytes, cosine_table)
+    own = lax.axis_index("dp").astype(jnp.int32).reshape(1)
+    update = summed_update(own, all_values.transpose(0, 2, 1), all_bytes, cosine_table)
     return (
         gate_grad,
         up_grad,

time: 153 us -> 183 us (1.20)
  blocking collectives: 73.4 us -> 10.1 us
  starting transfers between devices: 6.33 us -> 60 us
  waiting for transfers between devices: 0.02 us -> 30.4 us
  other arithmetic: 16 us -> 21 us
  local copies, waits for them, and re-layouts: 17.6 us -> 21.7 us
    all_gather x4 -> x1, blocking collectives: 73.4 us -> 10.1 us  [per_device(): lax.all_gather(jnp.concatenate([by_worker, tail], axis=0), 'fsdp', axis=1...]
    ppermute x0 -> x6, starting transfers between devices: none -> 53.5 us  [from_each(): lax.ppermute(block, 'dp', [(i, (i + step) % workers) for i in range(worke...]
    ppermute x0 -> x6, waiting for transfers between devices: none -> 26.4 us  [from_each(): lax.ppermute(block, 'dp', [(i, (i + step) % workers) for i in range(worke...]
    ppermute x0 -> x3, local copies, waits for them, and re-layouts: none -> 6.73 us  [from_each(): lax.ppermute(block, 'dp', [(i, (i + step) % workers) for i in range(worke...]
    unnamed x20 -> x26, local copies, waits for them, and re-layouts: 7.24 us -> 2.3 us
    shift_right_arithmetic x1 -> x3, other arithmetic: 0.19 us -> 4.61 us  [group_bytes(): slots >> 3]
    shift_left x1 -> x4, local copies, waits for them, and re-layouts: 1.49 us -> 5.78 us  [group_bytes(): bits = jnp.left_shift(1, slots & 7)]
    all_to_all x1, waiting for transfers between devices: 0.01 us -> 3.95 us  [per_device(): lax.all_to_all(out_grad.reshape(token_rows, workers, features).transpose(...]
  transfers between devices with their start and end apart: 2 -> 8, of which waited for: 0 -> 3; matrix products, arithmetic and copies ran while one was open for 21% -> 22% of each run, Pallas kernels for 8% -> 6%
where the time goes in v3:
time: 183 us; the launch traced here: 182 us
  starting transfers between devices  60 us (33%)
  waiting for transfers between devices  30.4 us (17%)
  local copies, waits for them, and re-layouts  21.7 us (12%)
  other arithmetic  21 us (11%)
  between operations  14.3 us (8%)
  matrix products  12.4 us (7%)
  Pallas kernels  12.4 us (7%)
  blocking collectives  10.1 us (6%)
    ppermute x6, starting transfers between devices, from_each(): lax.ppermute(block, 'dp', [(i, (i + step) % workers) for i in range(worke...  53.5 us
    ppermute x6, waiting for transfers between devices, from_each(): lax.ppermute(block, 'dp', [(i, (i + step) % workers) for i in range(worke...  26.4 us
    pallas_call x1, Pallas kernels, summed_update(): pl.pallas_call(update_kernel, grid=(rows // tile,), out_shape=jax.ShapeDt...  10.8 us
    all_gather x1, blocking collectives, per_device(): lax.all_gather(jnp.concatenate([by_worker, tail], axis=0), 'fsdp', axis=1...  10.1 us
    ppermute x3, local copies, waits for them, and re-layouts, from_each(): lax.ppermute(block, 'dp', [(i, (i + step) % workers) for i in range(worke...  6.73 us
    reduce_sum x4, other arithmetic, group_bytes(): jnp.sum(jnp.where((slots >> 3)[..., None, :, :] == group[:, None, None],...  6.69 us
    all_to_all x1, starting transfers between devices, per_device(): lax.all_to_all(out_grad.reshape(token_rows, workers, features).transpose(...  6.46 us
    shift_left x4, local copies, waits for them, and re-layouts, group_bytes(): bits = jnp.left_shift(1, slots & 7)  5.78 us
  transfers between devices with their start and end apart: 8, of which 3 were waited for; matrix products, arithmetic and copies ran while one was open for 22% of the time, Pallas kernels for 6%

profile of v3, /device:TPU:0, one launch (start us, length us, event | category | flops | bytes accessed | tf_op | source)
XLA Modules:
  0.0 182.4 jit_solution(8211701702633377824)
XLA Ops:
  7.2 6.5 %all-to-all-start = ((bf16[4,8,1024]{2,1,0:T(8,128)(2,1)}), bf16[4,8,1024]{2,1,0:T(8,128)(2,1)S(1)}, u32[]{:S(2)}, u32[]{:S(2)}) async-start(bf16[4,8,1024]{2,1,0:T(8,128)(2,1)} %bitcast.47), calls=%async_computation | async-start | bytes 131072 | tf_op jit(solution)/shard_map/all_to_all | solution.py:170
  15.5 3.9 %all-to-all-done = bf16[4,8,1024]{2,1,0:T(8,128)(2,1)S(1)} async-done(((bf16[4,8,1024]{2,1,0:T(8,128)(2,1)}), bf16[4,8,1024]{2,1,0:T(8,128)(2,1)S(1)}, u32[]{:S(2)}, u32[]{:S(2)}) %all-to-all-start) | async-done | bytes 65568 | tf_op jit(solution)/shard_map/all_to_all | solution.py:170
  19.4 10.1 %all_gather.3 = bf16[5,64,1024]{2,1,0:T(8,128)(2,1)S(1)} all-gather(bf16[5,8,1024]{2,1,0:T(8,128)(2,1)S(1)} %pad_maximum_fusion.1), channel_id=1, replica_groups=mesh['dp'=4,'fsdp'=8] {'fsdp'}, dimensions={1}, use_global_device_ids=true | all-gather | bytes 737280 | tf_op jit(solution)/shard_map/all_gather | solution.py:180
  32.2 2.6 %fusion.19.spectrum_ref = f32[1856,256]{1,0:T(8,128)S(1)} fusion(f32[1856,256]{1,0:T(8,128)S(1)} %fusion, f32[256]{0:T(256)S(1)} %get-tuple-element.26, f32[256]{0:T(256)S(1)} %iota_convert_fusion, f32[256]{0:T(256)S(1)} %get-tuple-element.27), kind=kOutput, calls=%fused_computation.56 | convolution fusion | flops 1459814400 | bytes 3804160 | tf_op jit(solution)/shard_map/dot_general | solution.py:233
  37.4 1.5 minimum_convert_fusion
  39.0 1.6 shard_map.102
  43.4 1.6 collective-permute-start.1
  45.4 3.4 %collective-permute-start.5 = (bf16[32,1856]{0,1:T(8,128)(2,1)}, bf16[32,1856]{0,1:T(8,128)(2,1)}, u32[]{:S(2)}, u32[]{:S(2)}) collective-permute-start(bf16[32,1856]{0,1:T(8,128)(2,1)} %get-tuple-element.12), channel_id=1, source_target_pairs={{0,24},{8,0},{16,8},{24,16},{1,25},{9,1},{17,9},{25,17},{2,26},{10... | collective-permute-start | bytes 356360 | tf_op jit(solution)/shard_map/ppermute | solution.py:63
  48.9 4.8 %fusion.35 = f32[256,1856]{1,0:T(8,128)} fusion(bf16[256,1024]{1,0:T(8,128)(2,1)} %bitcast.46, bf16[1856,1024]{1,0:T(8,128)(2,1)} %param.10), kind=kOutput, calls=%fused_computation.86 | convolution fusion | flops 973078528 | bytes 6225920 | tf_op jit(solution)/shard_map/dot_general | solution.py:183
  53.7 2.3 %copy.52 = s32[32,1856]{1,0:T(8,128)} copy(s32[32,1856]{0,1:T(8,128)} %get-tuple-element.13) | data formatting | bytes 475136 | tf_op jit(solution)/shard_map/shift_left | solution.py:37
  57.0 2.2 %select_reduce_fusion.3 = s32[32,1856]{1,0:T(8,128)S(1)} fusion(s32[32,1856]{1,0:T(8,128)} %copy.52, s32[32,1856]{1,0:T(8,128)} %copy.51), kind=kLoop, calls=%fused_computation.6 | loop fusion | flops 5642240 | bytes 712704 | tf_op jit(solution)/shard_map/reduce_sum | solution.py:38
  60.8 3.9 %fusion.1 = f32[1,1856,256]{2,1,0:T(8,128)} fusion(f32[1856,256]{1,0:T(8,128)S(1)} %copy-done.1, f32[1856,256]{1,0:T(8,128)S(1)} %fusion.5, f32[256]{0:T(256)S(1)} %get-tuple-element.26, f32[256]{0:T(256)S(1)} %iota_convert_fusion, f32[256]{0:T(256)S(1)} %get-tuple-element.27), kind=kOutput, calls=%fused_computation.15 | convolution fusion | flops 1460289536 | bytes 5704704 | tf_op jit(solution)/shard_map/dot_general | solution.py:237
  64.7 17.6 %collective-permute-done.5 = bf16[32,1856]{0,1:T(8,128)(2,1)} collective-permute-done((bf16[32,1856]{0,1:T(8,128)(2,1)}, bf16[32,1856]{0,1:T(8,128)(2,1)}, u32[]{:S(2)}, u32[]{:S(2)}) %collective-permute-start.5) | collective-permute-done | bytes 118816 | tf_op jit(solution)/shard_map/ppermute | solution.py:63
  82.4 47.3 %collective-permute-start.3 = (bf16[32,1856]{0,1:T(8,128)(2,1)}, bf16[32,1856]{0,1:T(8,128)(2,1)}, u32[]{:S(2)}, u32[]{:S(2)}) collective-permute-start(bf16[32,1856]{0,1:T(8,128)(2,1)} %get-tuple-element.12), channel_id=1, source_target_pairs={{0,8},{8,16},{16,24},{24,0},{1,9},{9,17},{17,25},{25,1},{2,10},{10... | collective-permute-start | bytes 356360 | tf_op jit(solution)/shard_map/ppermute | solution.py:63
  130.9 8.8 %collective-permute-done.4 = bf16[32,1856]{0,1:T(8,128)(2,1)} collective-permute-done((bf16[32,1856]{0,1:T(8,128)(2,1)}, bf16[32,1856]{0,1:T(8,128)(2,1)}, u32[]{:S(2)}, u32[]{:S(2)}) %collective-permute-start.4) | collective-permute-done | bytes 118816 | tf_op jit(solution)/shard_map/ppermute | solution.py:63
  139.7 2.1 %convert_shift-right-arithmetic_fusion.1 = (s32[32,1856]{0,1:T(8,128)S(1)}, s32[32,1856]{0,1:T(8,128)}) fusion(bf16[32,1856]{0,1:T(8,128)(2,1)} %collective-permute-done.4), kind=kLoop, calls=%fused_computation.24 | loop fusion | flops 237568 | bytes 593920 | tf_op jit(solution)/shard_map/shift_right_arithmetic | solution.py:40
  143.2 1.5 copy.62
  149.4 2.1 %select_reduce_fusion.1 = s32[32,1856]{1,0:T(8,128)S(1)} fusion(s32[32,1856]{1,0:T(8,128)S(1)} %copy.62, s32[32,1856]{1,0:T(8,128)} %copy.61), kind=kLoop, calls=%fused_computation.2 | loop fusion | flops 5642240 | bytes 712704 | tf_op jit(solution)/shard_map/reduce_sum | solution.py:38
  153.9 2.3 %copy.58 = f32[32,1856]{0,1:T(8,128)} copy(f32[32,1856]{1,0:T(8,128)} %collective-permute-done.2) | data formatting | bytes 475136 | tf_op jit(solution)/shard_map/ppermute | solution.py:63
  156.2 2.2 %copy.56 = f32[32,1856]{0,1:T(8,128)} copy(f32[32,1856]{1,0:T(8,128)} %collective-permute-done.1) | data formatting | bytes 475136 | tf_op jit(solution)/shard_map/ppermute | solution.py:63
  158.4 2.2 %copy.54 = f32[32,1856]{0,1:T(8,128)} copy(f32[32,1856]{1,0:T(8,128)} %collective-permute-done) | data formatting | bytes 475136 | tf_op jit(solution)/shard_map/ppermute | solution.py:63
  160.6 2.0 %maximum_bitcast_fusion.values_ref = f32[4,1856,32]{2,1,0:T(8,128)S(1)} fusion(f32[1,32,1856]{1,2,0:T(8,128)} %bitcast.43, f32[1,32,1856]{1,2,0:T(8,128)} %bitcast.44, f32[1,32,1856]{1,2,0:T(8,128)} %bitcast.45, f32[1,32,1856]{1,2,0:T(8,128)S(1)} %copy-done.3), kind=kLoop, calls=%fused_computation.11 | loop fusion | flops 712704 | bytes 1900544 | tf_op jit(solution)/shard_map/transpose | solution.py:241
  162.6 10.8 %shard_map.103 = f32[1856,256]{1,0:T(8,128)} custom-call(s32[1]{0:T(128)} %bitcast.9.own_ref, f32[4,1856,32]{2,1,0:T(8,128)S(1)} %maximum_bitcast_fusion.values_ref, bf16[4,1856,32]{2,1,0:T(8,128)(2,1)S(1)} %bitcast.42, bf16[32,256]{1,0:T(8,128)(2,1)S(1)} %fusion.30.spread_ref, bf16[256,256]{1,0:T(8,128)(2,1)S(1)} %fusion.17.below_ref, ...), custom_call_target="tpu_custom_call" | custom-call | flops 1946157056 | bytes 7602176 | tf_op jit(solution)/shard_map/pallas_call | solution.py:140
  173.5 2.1 %multiply_convert_fusion = (bf16[64,1856]{1,0:T(8,128)(2,1)}, bf16[64,1856]{1,0:T(8,128)(2,1)}) fusion(f32[64,1856]{1,0:T(8,128)} %reduce-scatter.2.cloned.1.call-done, bf16[64,1856]{1,0:T(8,128)(2,1)S(1)} %copy-done.8, bf16[64,1856]{1,0:T(8,128)(2,1)S(1)} %copy-done.10), kind=kLoop, calls=%fused_computation.50 | loop fusion | flops 1781760 | bytes 1425408 | tf_op jit(solution)/shard_map/convert_element_type | solution.py:218
  (72 shorter events, 22.3 us)
Async XLA Ops:
  7.2 23.2 %copy-start.4 = (f32[1,1856,256]{2,1,0:T(8,128)S(1)}, f32[1,1856,256]{2,1,0:T(8,128)}, u32[]{:S(2)}) copy-start(f32[1,1856,256]{2,1,0:T(8,128)} %param.11) | copy-start | bytes 5701636
  7.2 23.2 %copy-start.7 = (bf16[64,1856]{1,0:T(8,128)(2,1)S(1)}, bf16[64,1856]{1,0:T(8,128)(2,1)}, u32[]{:S(2)}) copy-start(bf16[64,1856]{1,0:T(8,128)(2,1)} %param.8) | copy-start | bytes 712708
  7.2 23.2 %copy-start.9 = (bf16[64,1856]{1,0:T(8,128)(2,1)S(1)}, bf16[64,1856]{1,0:T(8,128)(2,1)}, u32[]{:S(2)}) copy-start(bf16[64,1856]{1,0:T(8,128)(2,1)} %param.9) | copy-start | bytes 712708
  7.2 12.2 %all-to-all-start = ((bf16[4,8,1024]{2,1,0:T(8,128)(2,1)}), bf16[4,8,1024]{2,1,0:T(8,128)(2,1)S(1)}, u32[]{:S(2)}, u32[]{:S(2)}) async-start(bf16[4,8,1024]{2,1,0:T(8,128)(2,1)} %bitcast.47), calls=%async_computation | async-start | bytes 131072 | tf_op jit(solution)/shard_map/all_to_all | solution.py:170
  13.7 159.8 %reduce-scatter.2.cloned.1.call-start = ((), (), s32[]{:S(2)}) async-start(), calls=%async_computation.2 | async-start | bytes 2457600 | tf_op jit(solution)/shard_map/reduce_scatter | solution.py:192
  30.9 1.3 copy-start
  32.2 2.6 %copy-start.12 = (s32[1,1856]{1,0:T(1,128)S(1)}, s32[1,1856]{1,0:T(1,128)}, u32[]{:S(2)}) copy-start(s32[1,1856]{1,0:T(1,128)} %param.13) | copy-start | bytes 22276
  32.2 2.7 %copy-start.11 = (s32[1,1856,32]{1,2,0:T(8,128)S(1)}, s32[1,1856,32]{1,2,0:T(8,128)}, u32[]{:S(2)}) copy-start(s32[1,1856,32]{1,2,0:T(8,128)} %param.12) | copy-start | bytes 712708
  42.7 111.2 %collective-permute-start.2 = (f32[32,1856]{1,0:T(8,128)}, f32[32,1856]{1,0:T(8,128)}, u32[]{:S(2)}, u32[]{:S(2)}) collective-permute-start(f32[32,1856]{1,0:T(8,128)} %copy.53), channel_id=1, source_target_pairs={{0,24},{8,0},{16,8},{24,16},{1,25},{9,1},{17,9},{25,17},{2,26},{10... | collective-permute-start | bytes 712712 | tf_op jit(solution)/shard_map/ppermute | solution.py:63
  43.4 112.7 %collective-permute-start.1 = (f32[32,1856]{1,0:T(8,128)}, f32[32,1856]{1,0:T(8,128)}, u32[]{:S(2)}, u32[]{:S(2)}) collective-permute-start(f32[32,1856]{1,0:T(8,128)} %copy.53), channel_id=1, source_target_pairs={{0,16},{8,24},{16,0},{24,8},{1,17},{9,25},{17,1},{25,9},{2,18},{10... | collective-permute-start | bytes 712712 | tf_op jit(solution)/shard_map/ppermute | solution.py:63
  45.0 113.3 %collective-permute-start = (f32[32,1856]{1,0:T(8,128)}, f32[32,1856]{1,0:T(8,128)}, u32[]{:S(2)}, u32[]{:S(2)}) collective-permute-start(f32[32,1856]{1,0:T(8,128)} %copy.53), channel_id=1, source_target_pairs={{0,8},{8,16},{16,24},{24,0},{1,9},{9,17},{17,25},{25,1},{2,10},{10... | collective-permute-start | bytes 712712 | tf_op jit(solution)/shard_map/ppermute | solution.py:63
  45.4 37.0 %collective-permute-start.5 = (bf16[32,1856]{0,1:T(8,128)(2,1)}, bf16[32,1856]{0,1:T(8,128)(2,1)}, u32[]{:S(2)}, u32[]{:S(2)}) collective-permute-start(bf16[32,1856]{0,1:T(8,128)(2,1)} %get-tuple-element.12), channel_id=1, source_target_pairs={{0,24},{8,0},{16,8},{24,16},{1,25},{9,1},{17,9},{25,17},{2,26},{10... | collective-permute-start | bytes 356360 | tf_op jit(solution)/shard_map/ppermute | solution.py:63
  48.9 90.8 %collective-permute-start.4 = (bf16[32,1856]{0,1:T(8,128)(2,1)}, bf16[32,1856]{0,1:T(8,128)(2,1)}, u32[]{:S(2)}, u32[]{:S(2)}) collective-permute-start(bf16[32,1856]{0,1:T(8,128)(2,1)} %get-tuple-element.12), channel_id=1, source_target_pairs={{0,16},{8,24},{16,0},{24,8},{1,17},{9,25},{17,1},{25,9},{2,18},{10... | collective-permute-start | bytes 356360 | tf_op jit(solution)/shard_map/ppermute | solution.py:63
  53.7 2.3 %copy-start.2 = (s32[32,1856]{0,1:T(8,128)S(1)}, s32[32,1856]{0,1:T(8,128)}, u32[]{:S(2)}) copy-start(s32[32,1856]{0,1:T(8,128)} %get-tuple-element.15) | copy-start | bytes 712708
  59.3 1.6 copy-start.1
  82.4 63.3 %collective-permute-start.3 = (bf16[32,1856]{0,1:T(8,128)(2,1)}, bf16[32,1856]{0,1:T(8,128)(2,1)}, u32[]{:S(2)}, u32[]{:S(2)}) collective-permute-start(bf16[32,1856]{0,1:T(8,128)(2,1)} %get-tuple-element.12), channel_id=1, source_target_pairs={{0,8},{8,16},{16,24},{24,0},{1,9},{9,17},{17,25},{25,1},{2,10},{10... | collective-permute-start | bytes 356360 | tf_op jit(solution)/shard_map/ppermute | solution.py:63
  145.7 2.6 %copy-start.5 = (s32[32,1856]{1,0:T(8,128)S(1)}, s32[32,1856]{1,0:T(8,128)}, u32[]{:S(2)}) copy-start(s32[32,1856]{1,0:T(8,128)} %copy.64) | copy-start | bytes 712708
  147.9 3.6 %copy-start.6 = (s32[32,1856]{1,0:T(8,128)S(1)}, s32[32,1856]{1,0:T(8,128)}, u32[]{:S(2)}) copy-start(s32[32,1856]{1,0:T(8,128)} %copy.60) | copy-start | bytes 712708
  153.8 6.8 %copy-start.3 = (f32[1,32,1856]{1,2,0:T(8,128)S(1)}, f32[1,32,1856]{1,2,0:T(8,128)}, u32[]{:S(2)}) copy-start(f32[1,32,1856]{1,2,0:T(8,128)} %get-tuple-element.16) | copy-start | bytes 712708
  162.6 10.9 %copy-start.8 = (bf16[64,1856]{1,0:T(8,128)(2,1)S(1)}, bf16[64,1856]{1,0:T(8,128)(2,1)}, u32[]{:S(2)}) copy-start(bf16[64,1856]{1,0:T(8,128)(2,1)} %param.8) | copy-start | bytes 712708
  162.6 10.8 %copy-start.10 = (bf16[64,1856]{1,0:T(8,128)(2,1)S(1)}, bf16[64,1856]{1,0:T(8,128)(2,1)}, u32[]{:S(2)}) copy-start(bf16[64,1856]{1,0:T(8,128)(2,1)} %param.9) | copy-start | bytes 712708
Sparse Core Ops, SparseCore 0:
  53.9 71.2 reduce-scatter.1

commit v4 on v2

--- a/solution.py
+++ b/solution.py
@@ -172,7 +172,6 @@
     )
     mask = ((expanded.astype(jnp.int32) >> (frequency & 7)[None, :]) & 1) == 1
 
-    window_grad = lax.all_gather(out_grad[:, :window], "fsdp", axis=0, tiled=True)
     by_worker = lax.all_to_all(
         out_grad.reshape(token_rows, workers, features).transpose(1, 0, 2),
         "dp",
@@ -180,13 +179,21 @@
         concat_axis=0,
         tiled=True,
     )
-    all_grad = lax.all_gather(by_worker, "fsdp", axis=1, tiled=True)
+    extra = -(-window // features)
+    tail = jnp.pad(out_grad[:, :window], ((0, 0), (0, extra * features - window)))
+    tail = tail.reshape(token_rows, extra, features).transpose(1, 0, 2)
+    gathered = lax.all_gather(
+        jnp.concatenate([by_worker, tail], axis=0), "fsdp", axis=1, tiled=True
+    )
     partial_grad = lax.dot_general(
-        all_grad.reshape(workers * worker_rows, features),
+        gathered[:workers].reshape(workers * worker_rows, features),
         down_weight,
         (((1,), (1,)), ((), ())),
         preferred_element_type=jnp.float32,
     )
+    window_grad = jnp.concatenate([gathered[workers + i] for i in range(extra)], axis=1)
+    first = partial_grad[0, 0]
+    window_grad = jnp.where(first == first, window_grad[:, :window], 0)
     hidden_grad = lax.psum_scatter(partial_grad, "dp", scatter_dimension=0, tiled=True)
 
     gate_float = gate_pre.astype(jnp.float32)

time: 153 us -> 153 us (level)
  blocking collectives: 73.4 us -> 63.2 us
  local copies, waits for them, and re-layouts: 17.6 us -> 24.5 us
  matrix products: 12.2 us -> 13.8 us
    all_gather x2 -> x1, blocking collectives: 18.9 us -> 10.3 us  [per_device(): lax.all_gather(jnp.concatenate([by_worker, tail], axis=0), 'fsdp', axis=1...]
    unnamed x20 -> x30, local copies, waits for them, and re-layouts: 7.24 us -> 15.2 us
    all_gather x1, blocking collectives: 21.9 us -> 15.5 us  [per_device(): all_slots = lax.all_gather(slots.astype(jnp.bfloat16), 'dp', axis=0)]
    all_gather x1, blocking collectives: 32.6 us -> 37.4 us  [per_device(): all_values = lax.all_gather(picked, 'dp', axis=0)]
    transpose x2, local copies, waits for them, and re-layouts: 2.49 us -> 0.36 us  [per_device(): picked = pick(spectrum, places)[:, :slot_count].T]
    dot_general x1, matrix products: 0.48 us -> 2.26 us  [per_device(): lax.dot_general(hidden, window_grad, (((0,), (0,)), ((), ())), preferred_...]
    convert_element_type x1, other arithmetic: 2.05 us -> 0.5 us  [per_device(): up_grad = (hidden_grad * activation).astype(jnp.bfloat16)]
  transfers between devices with their start and end apart: 2 -> 2, of which waited for: 0 -> 0; matrix products, arithmetic and copies ran while one was open for 21% -> 25% of each run, Pallas kernels for 8% -> 8%
where the time goes in v4:
time: 153 us
  blocking collectives  63.2 us (41%)
  local copies, waits for them, and re-layouts  24.5 us (16%)
  other arithmetic  16.8 us (11%)
  between operations  15.6 us (10%)
  matrix products  13.8 us (9%)
  Pallas kernels  12.3 us (8%)
  starting transfers between devices  6.33 us (4%)
    all_gather x1, blocking collectives, per_device(): all_values = lax.all_gather(picked, 'dp', axis=0)  37.4 us
    all_gather x1, blocking collectives, per_device(): all_slots = lax.all_gather(slots.astype(jnp.bfloat16), 'dp', axis=0)  15.5 us
    unnamed x30, local copies, waits for them, and re-layouts  15.2 us
    pallas_call x1, Pallas kernels, summed_update(): pl.pallas_call(update_kernel, grid=(rows // tile,), out_shape=jax.ShapeDt...  10.7 us
    all_gather x1, blocking collectives, per_device(): lax.all_gather(jnp.concatenate([by_worker, tail], axis=0), 'fsdp', axis=1...  10.3 us
    reduce_sum x2, other arithmetic, group_bytes(): jnp.sum(jnp.where((slots >> 3)[..., None, :, :] == group[:, None, None],...  9.2 us
    all_to_all x1, starting transfers between devices, per_device(): lax.all_to_all(out_grad.reshape(token_rows, workers, features).transpose(...  6.33 us
    dot_general x1, matrix products, per_device(): lax.dot_general(gathered[:workers].reshape(workers * worker_rows, feature...  4.52 us
  transfers between devices with their start and end apart: 2, of which 0 were waited for; matrix products, arithmetic and copies ran while one was open for 25% of the time, Pallas kernels for 8%

profile of v4, /device:TPU:0, one launch (start us, length us, event | category | flops | bytes accessed | tf_op | source)
XLA Modules:
  0.0 152.5 jit_solution(14799063313732388011)
XLA Ops:
  7.2 6.3 %all-to-all-start = ((bf16[4,8,1024]{2,1,0:T(8,128)(2,1)}), bf16[4,8,1024]{2,1,0:T(8,128)(2,1)S(1)}, u32[]{:S(2)}, u32[]{:S(2)}) async-start(bf16[4,8,1024]{2,1,0:T(8,128)(2,1)} %bitcast.37), calls=%async_computation | async-start | bytes 131072 | tf_op jit(solution)/shard_map/all_to_all | solution.py:175
  16.1 1.4 select_reduce_fusion.2
  17.7 1.2 minimum_convert_fusion
  19.1 15.5 %all-gather.1 = bf16[128,1856]{1,0:T(8,128)(2,1)S(1)} all-gather(bf16[32,1856]{1,0:T(8,128)(2,1)S(1)} %copy.57), channel_id=3, replica_groups=mesh['dp'=4,'fsdp'=8] {'dp'}, dimensions={0}, use_global_device_ids=true | all-gather | bytes 593920 | tf_op jit(solution)/shard_map/all_gather | solution.py:163
  34.8 6.4 %select_reduce_fusion = s32[4,32,1856]{2,1,0:T(8,128)S(1)} fusion(s32[4,32,1856]{2,1,0:T(8,128)S(1)} %bitcast.35, s32[4,32,1856]{2,1,0:T(8,128)S(1)} %bitcast.34), kind=kLoop, calls=%fused_computation | loop fusion | flops 22568960 | bytes 2850816 | tf_op jit(solution)/shard_map/reduce_sum | solution.py:38
  41.9 1.2 copy.50
  43.1 2.1 %copy.49 = bf16[64,1856]{0,1:T(8,128)(2,1)} copy(bf16[64,1856]{1,0:T(8,128)(2,1)} %param.9) | data formatting | bytes 475136 | tf_op args[2]
  47.3 1.7 %copy.58 = bf16[4,32,1856]{1,2,0:T(8,128)(2,1)} copy(bf16[4,32,1856]{2,1,0:T(8,128)(2,1)S(1)} %convert_element_type.89) | data formatting | bytes 950272 | tf_op jit(solution)/shard_map/convert_element_type | solution.py:43
  49.1 10.3 %all_gather.13 = bf16[5,64,1024]{2,1,0:T(8,128)(2,1)S(1)} all-gather(bf16[5,8,1024]{2,1,0:T(8,128)(2,1)S(1)} %pad_maximum_fusion), channel_id=1, replica_groups=mesh['dp'=4,'fsdp'=8] {'fsdp'}, dimensions={1}, use_global_device_ids=true | all-gather | bytes 737280 | tf_op jit(solution)/shard_map/all_gather | solution.py:185
  59.5 4.5 %fusion.35 = f32[256,1856]{0,1:T(8,128)} fusion(bf16[256,1024]{1,0:T(8,128)(2,1)S(1)} %bitcast.36, bf16[1856,1024]{1,0:T(8,128)(2,1)} %param.10), kind=kOutput, calls=%fused_computation.72 | convolution fusion | flops 973078528 | bytes 6225920 | tf_op jit(solution)/shard_map/dot_general | solution.py:188
  64.0 2.9 %copy.61 = f32[256,1856]{1,0:T(8,128)} copy(f32[256,1856]{0,1:T(8,128)} %fusion.35) | data formatting | bytes 3801088
  68.0 2.8 %select_reduce_fusion.1 = s32[32,1856]{1,0:T(8,128)} fusion(s32[32,1856]{1,0:T(8,128)S(1)} %copy-done.9, s32[32,1856]{1,0:T(8,128)} %copy.53), kind=kLoop, calls=%fused_computation.2 | loop fusion | flops 5642240 | bytes 712704 | tf_op jit(solution)/shard_map/reduce_sum | solution.py:38
  70.8 1.2 slice.26
  73.3 2.3 %fusion = f32[1856,256]{1,0:T(8,128)S(1)} fusion(f32[1,1856,256]{2,1,0:T(8,128)} %param.11, bf16[64,1856]{0,1:T(8,128)(2,1)S(1)} %copy-done.7, bf16[64,1856]{0,1:T(8,128)(2,1)S(1)} %copy.50, bf16[64,1024]{1,0:T(8,128)(2,1)S(1)} %slice_bitcast_fusion.1, pred[]{:T(512)} %bitcast.5), kind=kOutput, calls=%fused_computation.9 | convolution fusion | flops 63209472 | bytes 4784129 | tf_op jit(solution)/shard_map/dot_general | solution.py:211
  75.6 1.2 copy-done.2
  76.8 2.6 %fusion.17.spectrum_ref = f32[1856,256]{1,0:T(8,128)S(1)} fusion(f32[1856,256]{1,0:T(8,128)S(1)} %fusion, f32[256]{0:T(256)S(1)} %get-tuple-element.32, f32[256]{0:T(256)S(1)} %iota_convert_fusion, f32[256]{0:T(256)S(1)} %get-tuple-element.33), kind=kOutput, calls=%fused_computation.43 | convolution fusion | flops 1459814400 | bytes 3804160 | tf_op jit(solution)/shard_map/dot_general | solution.py:219
  79.4 1.6 %shard_map.102 = f32[1856,128]{1,0:T(8,128)S(1)} custom-call(f32[1856,256]{1,0:T(8,128)S(1)} %fusion.17.spectrum_ref, s32[1856,128]{1,0:T(8,128)S(1)} %pad.9.places_ref), custom_call_target="tpu_custom_call" | custom-call | flops 1900544 | bytes 3801088 | tf_op jit(solution)/shard_map/pallas_call | solution.py:78
  81.4 37.4 %all-gather = f32[128,1856]{1,0:T(8,128)} all-gather(f32[32,1856]{1,0:T(8,128)S(1)} %copy.55), channel_id=2, replica_groups=mesh['dp'=4,'fsdp'=8] {'dp'}, dimensions={0}, use_global_device_ids=true | all-gather | bytes 1187840 | tf_op jit(solution)/shard_map/all_gather | solution.py:221
  118.8 3.4 %copy.56 = f32[4,32,1856]{1,2,0:T(8,128)} copy(f32[4,32,1856]{2,1,0:T(8,128)} %bitcast.33) | data formatting | bytes 1900544 | tf_op jit(solution)/shard_map/all_gather | solution.py:221
  122.2 2.1 %copy-done = f32[4,32,1856]{1,2,0:T(8,128)S(1)} copy-done((f32[4,32,1856]{1,2,0:T(8,128)S(1)}, f32[4,32,1856]{1,2,0:T(8,128)}, u32[]{:S(2)}) %copy-start) | copy-done | bytes 950296
  124.3 1.6 %copy-done.1 = bf16[4,32,1856]{1,2,0:T(8,128)(2,1)S(1)} copy-done((bf16[4,32,1856]{1,2,0:T(8,128)(2,1)S(1)}, bf16[4,32,1856]{1,2,0:T(8,128)(2,1)}, u32[]{:S(2)}) %copy-start.1) | copy-done | bytes 475160
  125.9 10.7 %shard_map.103 = f32[1856,256]{1,0:T(8,128)} custom-call(f32[4,1856,32]{2,1,0:T(8,128)S(1)} %bitcast.31, bf16[4,1856,32]{2,1,0:T(8,128)(2,1)S(1)} %bitcast.32, bf16[32,256]{1,0:T(8,128)(2,1)S(1)} %fusion.27.spread_ref, bf16[256,256]{1,0:T(8,128)(2,1)S(1)} %fusion.16.below_ref, f32[256,256]{1,0:T(8,128)S(1)} %cosine_multiply_fusion.table_ref), custom_call_target="tpu_custom_call" | custom-call | flops 1946157056 | bytes 7602176 | tf_op jit(solution)/shard_map/pallas_call | solution.py:132
  138.1 3.9 %fusion.1 = f32[1,1856,256]{2,1,0:T(8,128)} fusion(f32[1856,256]{1,0:T(8,128)S(1)} %copy-done.3, f32[1856,256]{1,0:T(8,128)S(1)} %fusion.5, f32[256]{0:T(256)S(1)} %get-tuple-element.32, f32[256]{0:T(256)S(1)} %iota_convert_fusion, f32[256]{0:T(256)S(1)} %get-tuple-element.33), kind=kOutput, calls=%fused_computation.10 | convolution fusion | flops 1460289536 | bytes 5704704 | tf_op jit(solution)/shard_map/dot_general | solution.py:223
  142.0 1.3 copy.62
  (53 shorter events, 11.4 us)
Async XLA Ops:
  7.2 41.9 %all-to-all-start = ((bf16[4,8,1024]{2,1,0:T(8,128)(2,1)}), bf16[4,8,1024]{2,1,0:T(8,128)(2,1)S(1)}, u32[]{:S(2)}, u32[]{:S(2)}) async-start(bf16[4,8,1024]{2,1,0:T(8,128)(2,1)} %bitcast.37), calls=%async_computation | async-start | bytes 131072 | tf_op jit(solution)/shard_map/all_to_all | solution.py:175
  13.5 128.5 %reduce-scatter.4.cloned.1.call-start = ((), (), s32[]{:S(2)}) async-start(), calls=%async_computation.2 | async-start | bytes 2457600
  34.8 6.4 %copy-start.11 = (pred[1024]{0:T(1024)(128)(4,1)S(1)}, pred[1024]{0:T(1024)(128)(4,1)}, u32[]{:S(2)}) copy-start(pred[1024]{0:T(1024)(128)(4,1)} %constant.16.clone.1) | copy-start | bytes 3076
  43.1 30.2 %copy-start.5 = (bf16[64,1856]{0,1:T(8,128)(2,1)}, bf16[64,1856]{0,1:T(8,128)(2,1)S(1)}, u32[]{:S(2)}) copy-start(bf16[64,1856]{0,1:T(8,128)(2,1)S(1)} %copy.50) | copy-start | bytes 712708
  47.3 1.7 %copy-start.4 = (s32[1856,32]{1,0:T(8,128)S(1)}, s32[1856,32]{1,0:T(8,128)}, u32[]{:S(2)}) copy-start(s32[1856,32]{1,0:T(8,128)} %get-tuple-element.28) | copy-start | bytes 712708
  66.9 1.1 copy-start.9
  66.9 6.4 %copy-start.7 = (bf16[64,1856]{0,1:T(8,128)(2,1)S(1)}, bf16[64,1856]{0,1:T(8,128)(2,1)}, u32[]{:S(2)}) copy-start(bf16[64,1856]{0,1:T(8,128)(2,1)} %copy.49) | copy-start | bytes 712708
  75.6 1.3 copy-start.2
  122.2 2.1 %copy-start = (f32[4,32,1856]{1,2,0:T(8,128)S(1)}, f32[4,32,1856]{1,2,0:T(8,128)}, u32[]{:S(2)}) copy-start(f32[4,32,1856]{1,2,0:T(8,128)} %copy.56) | copy-start | bytes 2850820
  124.3 1.6 %copy-start.1 = (bf16[4,32,1856]{1,2,0:T(8,128)(2,1)S(1)}, bf16[4,32,1856]{1,2,0:T(8,128)(2,1)}, u32[]{:S(2)}) copy-start(bf16[4,32,1856]{1,2,0:T(8,128)(2,1)} %copy.58) | copy-start | bytes 1425412
  125.9 10.7 %copy-start.10 = (s32[32,1856]{1,0:T(8,128)S(1)}, s32[32,1856]{1,0:T(8,128)}, u32[]{:S(2)}) copy-start(s32[32,1856]{1,0:T(8,128)} %select_reduce_fusion.1) | copy-start | bytes 712708
  136.6 1.5 copy-start.3
  138.1 5.2 %copy-start.6 = (bf16[64,1856]{0,1:T(8,128)(2,1)S(1)}, bf16[64,1856]{0,1:T(8,128)(2,1)}, u32[]{:S(2)}) copy-start(bf16[64,1856]{0,1:T(8,128)(2,1)} %copy-done.5) | copy-start | bytes 712708
  138.1 5.3 %copy-start.8 = (bf16[64,1856]{0,1:T(8,128)(2,1)S(1)}, bf16[64,1856]{0,1:T(8,128)(2,1)}, u32[]{:S(2)}) copy-start(bf16[64,1856]{0,1:T(8,128)(2,1)} %copy.49) | copy-start | bytes 712708
Sparse Core Ops, SparseCore 0:
  67.0 58.1 reduce-scatter.3
